TPU v7x, 128 devices: a whole 4x4x4 slice. The times are simulated.
128 devices in a mesh: dp: 32 (over z, x_lo, y), tensor: 4 (over x_hi, core).
Axes of the slice: x: 4 (x_hi: 2, x_lo: 2; x = x_hi * 2 + x_lo), y: 4, z: 4, core: 2. Of those that a mesh axis runs over, the one named last changes fastest.
Arguments:
- tokens: bfloat16 [16384, 1024], P(('dp', 'tensor')), may hold values from -6 to 6
- segment_ids: int32 [16384], P('dp'), may hold values from 0 to 3, as said below
- cotangent: bfloat16 [16384, 1024], P(('dp', 'tensor')), may hold values from -6 to 6
- attn_norm: float32 [2, 1024], replicated, may hold values from 0.1 to 1.9
- q_weight: bfloat16 [2, 1024, 2048], P(None, 'dp', 'tensor'), may hold values from -0.1875 to 0.1875
- key_projection: bfloat16 [2, 1024, 1024], P(None, 'dp', 'tensor'), may hold values from -0.1875 to 0.1875
- value_projection: bfloat16 [2, 1024, 1024], P(None, 'dp', 'tensor'), may hold values from -0.1875 to 0.1875
- o_weight: bfloat16 [2, 2048, 1024], P(None, 'tensor', 'dp'), may hold values from -1.5 to 1.5
- q_gain: float32 [2, 128], replicated, may hold values from 0.1 to 1.9
- k_gain: float32 [2, 128], replicated, may hold values from 0.1 to 1.9
- mlp_norm: float32 [2, 1024], replicated, may hold values from 0.1 to 1.9
- gate_weight: bfloat16 [2, 1024, 3072], P(None, 'dp', 'tensor'), may hold values from -0.1875 to 0.1875
- up_weight: bfloat16 [2, 1024, 3072], P(None, 'dp', 'tensor'), may hold values from -0.1875 to 0.1875
- down_weight: bfloat16 [2, 3072, 1024], P(None, 'tensor', 'dp'), may hold values from -0.109375 to 0.109375
Outputs:
- output: bfloat16 [16384, 1024], P(('dp', 'tensor'))
- input_grad: float32 [16384, 1024], P(('dp', 'tensor'))
- attn_norm_grad: float32 [2, 1024], replicated
- q_weight_grad: float32 [2, 1024, 2048], P(None, 'dp', 'tensor')
- k_weight_grad: float32 [2, 1024, 1024], P(None, 'dp', 'tensor')
- v_weight_grad: float32 [2, 1024, 1024], P(None, 'dp', 'tensor')
- o_weight_grad: float32 [2, 2048, 1024], P(None, 'tensor', 'dp')
- q_gain_grad: float32 [2, 128], replicated
- k_gain_grad: float32 [2, 128], replicated
- mlp_norm_grad: float32 [2, 1024], replicated
- gate_weight_grad: float32 [2, 1024, 3072], P(None, 'dp', 'tensor')
- up_weight_grad: float32 [2, 1024, 3072], P(None, 'dp', 'tensor')
- down_weight_grad: float32 [2, 3072, 1024], P(None, 'tensor', 'dp')
Inputs may be any that keep to these rules, and one draw needn't show every extreme that they name: `segment_ids`: in each group of 512 consecutive slots the ids never fall: documents 0, 1 and 2 (0 and 2 may be absent), then empty slots with id 3 up to the group's end; document 1 starts among the group's first 128 slots and ends among its last 128; in some group it fills all 512 slots.
All inputs are finite; a program needn't handle non-finite values.
Results may differ from a plain program's by a relative error of at most 0.04.
Values may be sent and summed in bfloat16 or wider, within the bound.
No kernel may reach another device: no remote copies, remote signals or barrier semaphores. Data moves between devices by JAX's collectives and lax.ppermute only.
A program may use at most 128 MiB of HBM per device.

v0:
```python
import math

import jax
import jax.numpy as jnp
from jax import lax
from jax.sharding import PartitionSpec as P

QUERY_HEADS = 16
KEY_VALUE_HEADS = 8
HEAD_SIZE = 128
DECODER_LAYERS = 2


NORM_EPS = 1e-06
ROPE_BASE = 1000000.0
MASK_FILL = -1000000000.0
QUERY_BLOCK = 512


def rms_scale(values, gain_vector):
    return (
        values
        * lax.rsqrt(jnp.mean(values * values, axis=-1, keepdims=True) + NORM_EPS)
        * gain_vector
    )


def rotary_tables(segment_ids):
    width = segment_ids.shape[0]
    column = jnp.arange(width, dtype=jnp.int32)
    doc_starts = jnp.zeros((width,), jnp.int32)
    for doc_number in range(4):
        before = jnp.sum((segment_ids < doc_number).astype(jnp.int32))
        doc_starts = doc_starts + jnp.where(segment_ids == doc_number, before, 0)
    position = (column - doc_starts).astype(jnp.float32)
    half_width = HEAD_SIZE // 2
    frequency = jnp.exp(
        jnp.arange(half_width, dtype=jnp.float32) * (-2.0 * math.log(ROPE_BASE) / HEAD_SIZE)
    )
    angles = position[:, None] * frequency[None, :]
    angles = jnp.concatenate([angles, angles], axis=-1)
    return (jnp.cos(angles)[:, None, :], jnp.sin(angles)[:, None, :])


def rotate(values, cosine_table, sine_table):
    half_width = values.shape[-1] // 2
    turned = jnp.concatenate([-values[..., half_width:], values[..., :half_width]], axis=-1)
    return values * cosine_table + turned * sine_table


def attention_mask(segment_ids):
    column = jnp.arange(segment_ids.shape[0], dtype=jnp.int32)
    same_doc = segment_ids[:, None] == segment_ids[None, :]
    causal = column[None, :] <= column[:, None]
    live_row = segment_ids[:, None] < 3
    return same_doc & causal & live_row | (column[:, None] == column[None, :])


def swiglu(gate_pre, up_pre):
    return jax.nn.silu(gate_pre) * up_pre


def block_scores(query_block, key_rot, mask_block):
    raw_scores = jnp.einsum(
        "qhgd,khd->hgqk", query_block, key_rot, preferred_element_type=jnp.float32
    )
    return jnp.where(mask_block[None, None], raw_scores * HEAD_SIZE ** (-0.5), MASK_FILL)


def split_blocks(values, block_count, block_rows):
    return values.reshape((block_count, block_rows) + values.shape[1:])


def attend_forward(query_rotated, key_rot, value_reduced, allowed):
    slot_count = query_rotated.shape[0]
    block_rows = min(QUERY_BLOCK, slot_count)
    block_count = slot_count // block_rows

    def one_block(block_pair):
        scaled = block_scores(block_pair[0], key_rot, block_pair[1])
        row_peak = jnp.max(scaled, axis=-1, keepdims=True)
        exponent = jnp.exp(scaled - row_peak)
        row_total = jnp.sum(exponent, axis=-1, keepdims=True)
        probability = (exponent / row_total).astype(jnp.bfloat16)
        mixed_heads = jnp.einsum(
            "hgqk,khd->qhgd", probability, value_reduced, preferred_element_type=jnp.float32
        )
        return (mixed_heads, row_peak + jnp.log(row_total))

    mixed_heads, log_total = lax.map(
        one_block,
        (
            split_blocks(query_rotated, block_count, block_rows),
            split_blocks(allowed, block_count, block_rows),
        ),
    )
    return (mixed_heads.reshape(query_rotated.shape), log_total)


def attend_backward(query_rotated, key_rot, value_reduced, log_total, grad_mixed, allowed):
    slot_count = query_rotated.shape[0]
    block_rows = min(QUERY_BLOCK, slot_count)
    block_count = slot_count // block_rows

    def one_step(carried, block_items):
        query_block, grad_block, mask_block, total_block = block_items
        probability = jnp.exp(block_scores(query_block, key_rot, mask_block) - total_block)
        grad_prob = jnp.einsum(
            "qhgd,khd->hgqk", grad_block, value_reduced, preferred_element_type=jnp.float32
        )
        grad_value = jnp.einsum(
            "hgqk,qhgd->khd",
            probability.astype(jnp.bfloat16),
            grad_block,
            preferred_element_type=jnp.float32,
        )
        inner_sum = jnp.sum(probability * grad_prob, axis=-1, keepdims=True)
        grad_score = (probability * (grad_prob - inner_sum) * HEAD_SIZE ** (-0.5)).astype(
            jnp.bfloat16
        )
        grad_query = jnp.einsum(
            "hgqk,khd->qhgd", grad_score, key_rot, preferred_element_type=jnp.float32
        )
        grad_key = jnp.einsum(
            "hgqk,qhgd->khd", grad_score, query_block, preferred_element_type=jnp.float32
        )
        return ((carried[0] + grad_key, carried[1] + grad_value), grad_query)

    zero_keys = jnp.zeros(key_rot.shape, jnp.float32)
    sums, grad_query = lax.scan(
        one_step,
        (zero_keys, zero_keys),
        (
            split_blocks(query_rotated, block_count, block_rows),
            split_blocks(grad_mixed, block_count, block_rows),
            split_blocks(allowed, block_count, block_rows),
            log_total,
        ),
    )
    return (grad_query.reshape(query_rotated.shape), sums[0], sums[1])


def gather_rows(row_block):
    return lax.all_gather(row_block, "tensor", axis=0, tiled=True)


def gather_grads(row_block):
    return lax.all_gather(row_block, "tensor", axis=0, tiled=True)


def scatter_rows(term_fn, token_row_count):
    return lax.psum_scatter(
        term_fn(jnp.int32(0), lax.axis_size("tensor") * token_row_count).astype(jnp.bfloat16),
        "tensor",
        scatter_dimension=0,
        tiled=True,
    ).astype(jnp.float32)


def scatter_grads(term_fn, token_row_count):
    return lax.psum_scatter(
        term_fn(jnp.int32(0), lax.axis_size("tensor") * token_row_count).astype(jnp.bfloat16),
        "tensor",
        scatter_dimension=0,
        tiled=True,
    ).astype(jnp.float32)


def body(
    tokens,
    segment_ids,
    cotangent,
    attn_norm,
    q_weight,
    key_projection,
    value_projection,
    o_weight,
    q_gain,
    k_gain,
    mlp_norm,
    gate_weight,
    up_weight,
    down_weight,
):
    cosine_table, sine_table = rotary_tables(segment_ids)
    allowed = attention_mask(segment_ids)
    slot_count = segment_ids.shape[0]
    token_row_count = tokens.shape[0]
    heads_per_group = QUERY_HEADS // KEY_VALUE_HEADS
    residual = tokens.astype(jnp.float32)
    saved_layers = []
    for decoder_layer_index in range(DECODER_LAYERS):
        full_weights = (
            lax.all_gather(q_weight[decoder_layer_index], "dp", axis=0, tiled=True),
            lax.all_gather(key_projection[decoder_layer_index], "dp", axis=0, tiled=True),
            lax.all_gather(value_projection[decoder_layer_index], "dp", axis=0, tiled=True),
            lax.all_gather(o_weight[decoder_layer_index], "dp", axis=1, tiled=True),
            lax.all_gather(gate_weight[decoder_layer_index], "dp", axis=0, tiled=True),
            lax.all_gather(up_weight[decoder_layer_index], "dp", axis=0, tiled=True),
            lax.all_gather(down_weight[decoder_layer_index], "dp", axis=1, tiled=True),
        )
        wq_full, wk_full, wv_full, wo_full, wg_full, wu_full, wd_full = full_weights
        normed_all = gather_rows(
            rms_scale(residual, attn_norm[decoder_layer_index]).astype(jnp.bfloat16)
        )
        query_pre = jnp.dot(normed_all, wq_full, preferred_element_type=jnp.float32).reshape(
            slot_count, -1, HEAD_SIZE
        )
        key_before_rotary = jnp.dot(
            normed_all, wk_full, preferred_element_type=jnp.float32
        ).reshape(slot_count, -1, HEAD_SIZE)
        value_reduced = jnp.dot(normed_all, wv_full, preferred_element_type=jnp.float32).astype(
            jnp.bfloat16
        )
        value_reduced = value_reduced.reshape(slot_count, -1, HEAD_SIZE)
        local_kv = key_before_rotary.shape[1]
        query_rotated = rotate(
            rms_scale(query_pre, q_gain[decoder_layer_index]), cosine_table, sine_table
        )
        query_rotated = query_rotated.astype(jnp.bfloat16).reshape(
            slot_count, local_kv, heads_per_group, HEAD_SIZE
        )
        key_rot = rotate(
            rms_scale(key_before_rotary, k_gain[decoder_layer_index]), cosine_table, sine_table
        ).astype(jnp.bfloat16)
        mixed_heads, log_total = attend_forward(query_rotated, key_rot, value_reduced, allowed)
        mixed_low = mixed_heads.reshape(slot_count, -1).astype(jnp.bfloat16)

        def branch_term(first_row, num_rows):
            return jnp.dot(mixed_low, wo_full, preferred_element_type=jnp.float32)

        middle = residual + scatter_rows(branch_term, token_row_count)
        normed_two_all = gather_rows(
            rms_scale(middle, mlp_norm[decoder_layer_index]).astype(jnp.bfloat16)
        )
        gate_pre = jnp.dot(normed_two_all, wg_full, preferred_element_type=jnp.float32)
        up_pre = jnp.dot(normed_two_all, wu_full, preferred_element_type=jnp.float32)
        product_low = swiglu(gate_pre, up_pre).astype(jnp.bfloat16)

        def feed_term(first_row, num_rows):
            return jnp.dot(product_low, wd_full, preferred_element_type=jnp.float32)

        kept_weights = None
        saved_layers.append(
            (
                residual,
                middle,
                normed_all,
                normed_two_all,
                query_pre,
                key_before_rotary,
                query_rotated,
                key_rot,
                value_reduced,
                log_total,
                mixed_low,
                gate_pre,
                up_pre,
                product_low,
                kept_weights,
            )
        )
        residual = middle + scatter_rows(feed_term, token_row_count)
    output = residual.astype(jnp.bfloat16)
    grad_rows = cotangent.astype(jnp.float32)
    grads_by_layer = [None] * DECODER_LAYERS
    gains_by_layer = [None] * DECODER_LAYERS
    for decoder_layer_index in range(DECODER_LAYERS - 1, -1, -1):
        (
            residual_in,
            middle,
            normed_all,
            normed_two_all,
            query_pre,
            key_before_rotary,
            query_rotated,
            key_rot,
            value_reduced,
            log_total,
            mixed_low,
            gate_pre,
            up_pre,
            product_low,
            kept_weights,
        ) = saved_layers[decoder_layer_index]
        full_weights = (
            lax.all_gather(q_weight[decoder_layer_index], "dp", axis=0, tiled=True),
            lax.all_gather(key_projection[decoder_layer_index], "dp", axis=0, tiled=True),
            lax.all_gather(value_projection[decoder_layer_index], "dp", axis=0, tiled=True),
            lax.all_gather(o_weight[decoder_layer_index], "dp", axis=1, tiled=True),
            lax.all_gather(gate_weight[decoder_layer_index], "dp", axis=0, tiled=True),
            lax.all_gather(up_weight[decoder_layer_index], "dp", axis=0, tiled=True),
            lax.all_gather(down_weight[decoder_layer_index], "dp", axis=1, tiled=True),
        )
        wq_full, wk_full, wv_full, wo_full, wg_full, wu_full, wd_full = full_weights
        local_kv = key_before_rotary.shape[1]
        grad_out_all = gather_grads(grad_rows.astype(jnp.bfloat16))
        down_part = jnp.einsum(
            "sf,sd->fd", product_low, grad_out_all, preferred_element_type=jnp.float32
        )
        grad_product = jnp.einsum(
            "sd,fd->sf", grad_out_all, wd_full, preferred_element_type=jnp.float32
        )
        swiglu_back = jax.vjp(swiglu, gate_pre, up_pre)[1]
        grad_gate, grad_up = swiglu_back(grad_product)
        grad_gate_low = grad_gate.astype(jnp.bfloat16)
        grad_up_low = grad_up.astype(jnp.bfloat16)
        gate_part = jnp.einsum(
            "sd,sf->df", normed_two_all, grad_gate_low, preferred_element_type=jnp.float32
        )
        up_part = jnp.einsum(
            "sd,sf->df", normed_two_all, grad_up_low, preferred_element_type=jnp.float32
        )

        def feed_grad_term(first_row, num_rows):
            first_term = jnp.einsum(
                "sf,df->sd", grad_gate_low, wg_full, preferred_element_type=jnp.float32
            )
            return first_term + jnp.einsum(
                "sf,df->sd", grad_up_low, wu_full, preferred_element_type=jnp.float32
            )

        grad_normed_two = scatter_grads(feed_grad_term, token_row_count)
        norm_back_two = jax.vjp(rms_scale, middle, mlp_norm[decoder_layer_index])[1]
        grad_middle_part, mlp_gain_part = norm_back_two(grad_normed_two)
        grad_middle = grad_rows + grad_middle_part
        grad_branch_all = gather_grads(grad_middle.astype(jnp.bfloat16))
        o_part = jnp.einsum(
            "sf,sd->fd", mixed_low, grad_branch_all, preferred_element_type=jnp.float32
        )
        grad_mixed = jnp.einsum(
            "sd,fd->sf", grad_branch_all, wo_full, preferred_element_type=jnp.float32
        )
        grad_mixed = grad_mixed.astype(jnp.bfloat16).reshape(
            slot_count, local_kv, heads_per_group, HEAD_SIZE
        )
        grad_query_rot, grad_key_rot, grad_value = attend_backward(
            query_rotated, key_rot, value_reduced, log_total, grad_mixed, allowed
        )

        def head_norm(pre_heads, gain_vector):
            return rotate(rms_scale(pre_heads, gain_vector), cosine_table, sine_table)

        query_back = jax.vjp(head_norm, query_pre, q_gain[decoder_layer_index])[1]
        grad_query_pre, q_gain_part = query_back(grad_query_rot.reshape(slot_count, -1, HEAD_SIZE))
        key_back = jax.vjp(head_norm, key_before_rotary, k_gain[decoder_layer_index])[1]
        grad_key_pre, k_gain_part = key_back(grad_key_rot)
        grad_query_low = grad_query_pre.reshape(slot_count, -1).astype(jnp.bfloat16)
        grad_key_low = grad_key_pre.reshape(slot_count, -1).astype(jnp.bfloat16)
        grad_value_low = grad_value.reshape(slot_count, -1).astype(jnp.bfloat16)
        q_part = jnp.einsum(
            "sd,sf->df", normed_all, grad_query_low, preferred_element_type=jnp.float32
        )
        k_part = jnp.einsum(
            "sd,sf->df", normed_all, grad_key_low, preferred_element_type=jnp.float32
        )
        v_part = jnp.einsum(
            "sd,sf->df", normed_all, grad_value_low, preferred_element_type=jnp.float32
        )

        def attend_grad_term(first_row, num_rows):
            query_term = jnp.einsum(
                "sf,df->sd", grad_query_low, wq_full, preferred_element_type=jnp.float32
            )
            key_term = jnp.einsum(
                "sf,df->sd", grad_key_low, wk_full, preferred_element_type=jnp.float32
            )
            value_term = jnp.einsum(
                "sf,df->sd", grad_value_low, wv_full, preferred_element_type=jnp.float32
            )
            return query_term + key_term + value_term

        grad_normed = scatter_grads(attend_grad_term, token_row_count)
        norm_back_one = jax.vjp(rms_scale, residual_in, attn_norm[decoder_layer_index])[1]
        grad_in_part, attn_gain_part = norm_back_one(grad_normed)
        grad_rows = grad_middle + grad_in_part
        grads_by_layer[decoder_layer_index] = (
            lax.psum_scatter(
                q_part.astype(jnp.bfloat16), "dp", scatter_dimension=0, tiled=True
            ).astype(jnp.float32),
            lax.psum_scatter(
                k_part.astype(jnp.bfloat16), "dp", scatter_dimension=0, tiled=True
            ).astype(jnp.float32),
            lax.psum_scatter(
                v_part.astype(jnp.bfloat16), "dp", scatter_dimension=0, tiled=True
            ).astype(jnp.float32),
            lax.psum_scatter(
                o_part.astype(jnp.bfloat16), "dp", scatter_dimension=1, tiled=True
            ).astype(jnp.float32),
            lax.psum_scatter(
                gate_part.astype(jnp.bfloat16), "dp", scatter_dimension=0, tiled=True
            ).astype(jnp.float32),
            lax.psum_scatter(
                up_part.astype(jnp.bfloat16), "dp", scatter_dimension=0, tiled=True
            ).astype(jnp.float32),
            lax.psum_scatter(
                down_part.astype(jnp.bfloat16), "dp", scatter_dimension=1, tiled=True
            ).astype(jnp.float32),
        )
        gains_by_layer[decoder_layer_index] = (
            attn_gain_part,
            q_gain_part,
            k_gain_part,
            mlp_gain_part,
        )
    stacked = [
        jnp.stack(
            [
                grads_by_layer[decoder_layer_index][member]
                for decoder_layer_index in range(DECODER_LAYERS)
            ]
        )
        for member in range(7)
    ]
    q_stack, k_stack, v_stack, o_stack, gate_stack, up_stack, down_stack = stacked
    gain_stack = [
        jnp.stack(
            [
                gains_by_layer[decoder_layer_index][member]
                for decoder_layer_index in range(DECODER_LAYERS)
            ]
        )
        for member in range(4)
    ]
    attn_gain_stack, q_gain_stack, k_gain_stack, mlp_gain_stack = gain_stack
    attn_gain_sum, q_gain_sum, k_gain_sum, mlp_gain_sum = lax.psum(
        (attn_gain_stack, q_gain_stack, k_gain_stack, mlp_gain_stack), ("dp", "tensor")
    )
    return (
        output,
        grad_rows,
        attn_gain_sum,
        q_stack,
        k_stack,
        v_stack,
        o_stack,
        q_gain_sum,
        k_gain_sum,
        mlp_gain_sum,
        gate_stack,
        up_stack,
        down_stack,
    )


def solution(mesh):
    return jax.shard_map(
        body,
        mesh=mesh,
        in_specs=(
            P(("dp", "tensor"), None),
            P("dp"),
            P(("dp", "tensor"), None),
            P(),
            P(None, "dp", "tensor"),
            P(None, "dp", "tensor"),
            P(None, "dp", "tensor"),
            P(None, "tensor", "dp"),
            P(),
            P(),
            P(),
            P(None, "dp", "tensor"),
            P(None, "dp", "tensor"),
            P(None, "tensor", "dp"),
        ),
        out_specs=(
            P(("dp", "tensor"), None),
            P(("dp", "tensor"), None),
            P(),
            P(None, "dp", "tensor"),
            P(None, "dp", "tensor"),
            P(None, "dp", "tensor"),
            P(None, "tensor", "dp"),
            P(),
            P(),
            P(),
            P(None, "dp", "tensor"),
            P(None, "dp", "tensor"),
            P(None, "tensor", "dp"),
        ),
        check_vma=False,
    )
```

profile of v0, /device:TPU:0, one launch (start us, length us, event | category | flops | bytes accessed | tf_op | source)
XLA Modules:
  0.0 4362.8 jit_solution(13852934040019913241)
XLA Ops:
  23.7 85.8 %all-gather = bf16[1,1024,256]{2,1,0:T(8,128)(2,1)S(1)} all-gather(bf16[1,32,256]{2,1,0:T(8,128)(2,1)S(1)} %get-tuple-element.185), channel_id=2, replica_groups=mesh['dp'=32,'tensor'=4] {'dp'}, dimensions={1}, use_global_device_ids=true | all-gather | bytes 540672 | tf_op jit(solution)/shard_map/all_gather | solution.py:196
  109.5 78.3 %all-gather.1 = bf16[1,1024,256]{2,1,0:T(8,128)(2,1)S(1)} all-gather(bf16[1,32,256]{2,1,0:T(8,128)(2,1)S(1)} %get-tuple-element.183), channel_id=3, replica_groups=mesh['dp'=32,'tensor'=4] {'dp'}, dimensions={1}, use_global_device_ids=true | all-gather | bytes 540672 | tf_op jit(solution)/shard_map/all_gather | solution.py:195
  199.1 141.4 %all-gather.51.cloned.1.call-done = bf16[1,512,1024]{1,2,0:T(8,128)(2,1)} async-done(((bf16[1,512,32]{1,2,0:T(8,128)(2,1)}), bf16[1,512,1024]{1,2,0:T(8,128)(2,1)}) %all-gather.51.cloned.1.call-update) | async-done | bytes 1048592 | tf_op jit(solution)/shard_map/all_gather | solution.py:197
  344.4 31.0 reduce-scatter.23.cloned.1.call-done
  379.9 149.5 %all-gather.53.cloned.1.call-done = bf16[1,1024,768]{2,1,0:T(8,128)(2,1)} async-done(((bf16[1,32,768]{2,1,0:T(8,128)(2,1)}), bf16[1,1024,768]{2,1,0:T(8,128)(2,1)}) %all-gather.53.cloned.1.call-update) | async-done | bytes 1572880 | tf_op jit(solution)/shard_map/all_gather | solution.py:198
  529.4 22.9 all-gather.35.cloned.1.call-done
  552.4 3.9 fusion.54
  556.3 150.2 %all-gather.55.cloned.1.call-done = bf16[1,1024,768]{2,1,0:T(8,128)(2,1)} async-done(((bf16[1,32,768]{2,1,0:T(8,128)(2,1)}), bf16[1,1024,768]{2,1,0:T(8,128)(2,1)}) %all-gather.55.cloned.1.call-update) | async-done | bytes 1572880 | tf_op jit(solution)/shard_map/all_gather | solution.py:199
  706.5 4.3 multiply_convert_fusion.3
  710.8 150.4 %all-gather.57.cloned.1.call-done = bf16[1,768,1024]{1,2,0:T(8,128)(2,1)} async-done(((bf16[1,768,32]{1,2,0:T(8,128)(2,1)}), bf16[1,768,1024]{1,2,0:T(8,128)(2,1)}) %all-gather.57.cloned.1.call-update) | async-done | bytes 1572880 | tf_op jit(solution)/shard_map/all_gather | solution.py:200
  865.0 31.8 reduce-scatter.25.cloned.1.call-done
  900.2 88.3 %all-gather.7 = bf16[1,1024,256]{2,1,0:T(8,128)(2,1)} all-gather(bf16[1,32,256]{2,1,0:T(8,128)(2,1)S(1)} %get-tuple-element.184), channel_id=9, replica_groups=mesh['dp'=32,'tensor'=4] {'dp'}, dimensions={1}, use_global_device_ids=true | all-gather | bytes 540672 | tf_op jit(solution)/shard_map/all_gather | solution.py:196
  988.5 78.7 %all-gather.8 = bf16[1,1024,256]{2,1,0:T(8,128)(2,1)S(1)} all-gather(bf16[1,32,256]{2,1,0:T(8,128)(2,1)S(1)} %get-tuple-element.182), channel_id=10, replica_groups=mesh['dp'=32,'tensor'=4] {'dp'}, dimensions={1}, use_global_device_ids=true | all-gather | bytes 540672 | tf_op jit(solution)/shard_map/all_gather | solution.py:195
  1082.2 142.8 %all-gather.61.cloned.1.call-done = bf16[1,512,1024]{1,2,0:T(8,128)(2,1)} async-done(((bf16[1,512,32]{1,2,0:T(8,128)(2,1)}), bf16[1,512,1024]{1,2,0:T(8,128)(2,1)}) %all-gather.61.cloned.1.call-update) | async-done | bytes 1048592 | tf_op jit(solution)/shard_map/all_gather | solution.py:197
  1228.8 31.2 reduce-scatter.27.cloned.1.call-done
  1264.7 149.3 %all-gather.65.cloned.1.call-done = bf16[1,1024,768]{2,1,0:T(8,128)(2,1)} async-done(((bf16[1,32,768]{2,1,0:T(8,128)(2,1)}), bf16[1,1024,768]{2,1,0:T(8,128)(2,1)}) %all-gather.65.cloned.1.call-update) | async-done | bytes 1572880 | tf_op jit(solution)/shard_map/all_gather | solution.py:199
  1414.0 22.4 all-gather.39.cloned.1.call-done
  1440.3 150.1 %all-gather.63.cloned.1.call-done = bf16[1,1024,768]{2,1,0:T(8,128)(2,1)} async-done(((bf16[1,32,768]{2,1,0:T(8,128)(2,1)}), bf16[1,1024,768]{2,1,0:T(8,128)(2,1)}) %all-gather.63.cloned.1.call-update) | async-done | bytes 1572880 | tf_op jit(solution)/shard_map/all_gather | solution.py:198
  1594.2 18.5 all-gather.41.cloned.1.call-done
  1612.7 154.0 %all-gather.67.cloned.1.call-done = bf16[1,768,1024]{1,2,0:T(8,128)(2,1)} async-done(((bf16[1,768,32]{1,2,0:T(8,128)(2,1)}), bf16[1,768,1024]{1,2,0:T(8,128)(2,1)}) %all-gather.67.cloned.1.call-update) | async-done | bytes 1572880 | tf_op jit(solution)/shard_map/all_gather | solution.py:200
  1766.7 5.1 multiply_convert_fusion.1
  1775.9 31.8 reduce-scatter.31.cloned.1.call-done
  1811.5 19.9 all-gather.43.cloned.1.call-done
  1838.7 9.3 broadcast_multiply_fusion.1
  1848.0 9.1 fusion.25
  1869.2 27.5 reduce-scatter.33.cloned.1.call-done
  1897.8 32.9 reduce-scatter.29.cloned.1.call-done
  1933.3 20.1 all-gather.45.cloned.1.call-done
  1953.5 4.1 multiply_convert_fusion
  1961.7 31.3 reduce-scatter.35.cloned.1.call-done
  2033.9 9.2 broadcast_multiply_fusion
  2051.0 9.1 fusion.19
  2076.2 104.1 %reduce-scatter.65.cloned.1.call-done = bf16[768,32]{0,1:T(8,128)(2,1)} async-done(((bf16[768,1024]{0,1:T(8,128)(2,1)}), bf16[768,32]{0,1:T(8,128)(2,1)}) %reduce-scatter.65.cloned.1.call-update) | async-done | bytes 49168 | tf_op jit(solution)/shard_map/reduce_scatter | solution.py:396
  2180.3 160.7 %reduce-scatter.63.cloned.1.call-done = bf16[768,32]{0,1:T(8,128)(2,1)} async-done(((bf16[768,1024]{0,1:T(8,128)(2,1)}), bf16[768,32]{0,1:T(8,128)(2,1)}) %reduce-scatter.63.cloned.1.call-update) | async-done | bytes 49168 | tf_op jit(solution)/shard_map/reduce_scatter | solution.py:396
  2342.6 159.6 %reduce-scatter.61.cloned.1.call-done = bf16[32,768]{1,0:T(8,128)(2,1)} async-done(((bf16[1024,768]{1,0:T(8,128)(2,1)}), bf16[32,768]{1,0:T(8,128)(2,1)}) %reduce-scatter.61.cloned.1.call-update) | async-done | bytes 49168 | tf_op jit(solution)/shard_map/reduce_scatter | solution.py:393
  2502.2 160.7 %reduce-scatter.59.cloned.1.call-done = bf16[32,768]{1,0:T(8,128)(2,1)} async-done(((bf16[1024,768]{1,0:T(8,128)(2,1)}), bf16[32,768]{1,0:T(8,128)(2,1)}) %reduce-scatter.59.cloned.1.call-update) | async-done | bytes 49168 | tf_op jit(solution)/shard_map/reduce_scatter | solution.py:393
  2664.3 159.3 %reduce-scatter.57.cloned.1.call-done = bf16[32,768]{1,0:T(8,128)(2,1)} async-done(((bf16[1024,768]{1,0:T(8,128)(2,1)}), bf16[32,768]{1,0:T(8,128)(2,1)}) %reduce-scatter.57.cloned.1.call-update) | async-done | bytes 49168 | tf_op jit(solution)/shard_map/reduce_scatter | solution.py:390
  2823.6 160.4 %reduce-scatter.55.cloned.1.call-done = bf16[32,768]{1,0:T(8,128)(2,1)} async-done(((bf16[1024,768]{1,0:T(8,128)(2,1)}), bf16[32,768]{1,0:T(8,128)(2,1)}) %reduce-scatter.55.cloned.1.call-update) | async-done | bytes 49168 | tf_op jit(solution)/shard_map/reduce_scatter | solution.py:390
  2985.6 157.1 %reduce-scatter.49.cloned.1.call-done = bf16[32,256]{1,0:T(8,128)(2,1)} async-done(((bf16[1024,256]{1,0:T(8,128)(2,1)}), bf16[32,256]{1,0:T(8,128)(2,1)}) %reduce-scatter.49.cloned.1.call-update) | async-done | bytes 16400 | tf_op jit(solution)/shard_map/reduce_scatter | solution.py:384
  3142.7 158.3 %reduce-scatter.47.cloned.1.call-done = bf16[32,256]{1,0:T(8,128)(2,1)} async-done(((bf16[1024,256]{1,0:T(8,128)(2,1)}), bf16[32,256]{1,0:T(8,128)(2,1)}) %reduce-scatter.47.cloned.1.call-update) | async-done | bytes 16400 | tf_op jit(solution)/shard_map/reduce_scatter | solution.py:384
  3302.4 157.2 %reduce-scatter.45.cloned.1.call-done = bf16[32,256]{1,0:T(8,128)(2,1)} async-done(((bf16[1024,256]{1,0:T(8,128)(2,1)}), bf16[32,256]{1,0:T(8,128)(2,1)}) %reduce-scatter.45.cloned.1.call-update) | async-done | bytes 16400 | tf_op jit(solution)/shard_map/reduce_scatter | solution.py:381
  3459.6 158.5 %reduce-scatter.43.cloned.1.call-done = bf16[32,256]{1,0:T(8,128)(2,1)} async-done(((bf16[1024,256]{1,0:T(8,128)(2,1)}), bf16[32,256]{1,0:T(8,128)(2,1)}) %reduce-scatter.43.cloned.1.call-update) | async-done | bytes 16400 | tf_op jit(solution)/shard_map/reduce_scatter | solution.py:381
  3619.4 158.2 %reduce-scatter.53.cloned.1.call-done = bf16[512,32]{0,1:T(8,128)(2,1)} async-done(((bf16[512,1024]{0,1:T(8,128)(2,1)}), bf16[512,32]{0,1:T(8,128)(2,1)}) %reduce-scatter.53.cloned.1.call-update) | async-done | bytes 32784 | tf_op jit(solution)/shard_map/reduce_scatter | solution.py:387
  3777.7 159.2 %reduce-scatter.51.cloned.1.call-done = bf16[512,32]{0,1:T(8,128)(2,1)} async-done(((bf16[512,1024]{0,1:T(8,128)(2,1)}), bf16[512,32]{0,1:T(8,128)(2,1)}) %reduce-scatter.51.cloned.1.call-update) | async-done | bytes 32784 | tf_op jit(solution)/shard_map/reduce_scatter | solution.py:387
  3938.3 28.7 reduce-scatter.37.cloned.1.call-done
  3968.2 161.4 %reduce-scatter.41.cloned.1.call-done = bf16[32,512]{1,0:T(8,128)(2,1)} async-done(((bf16[1024,512]{1,0:T(8,128)(2,1)}), bf16[32,512]{1,0:T(8,128)(2,1)}) %reduce-scatter.41.cloned.1.call-update) | async-done | bytes 32784 | tf_op jit(solution)/shard_map/reduce_scatter | solution.py:378
  4129.6 159.4 %reduce-scatter.39.cloned.1.call-done = bf16[32,512]{1,0:T(8,128)(2,1)} async-done(((bf16[1024,512]{1,0:T(8,128)(2,1)}), bf16[32,512]{1,0:T(8,128)(2,1)}) %reduce-scatter.39.cloned.1.call-update) | async-done | bytes 32784 | tf_op jit(solution)/shard_map/reduce_scatter | solution.py:378
  4290.5 63.0 %all-reduce.8 = (f32[2,1024]{1,0:T(2,128)}, f32[2,128]{1,0:T(2,128)}, f32[2,128]{1,0:T(2,128)}, f32[2,1024]{1,0:T(2,128)}) all-reduce(f32[2,1024]{1,0:T(2,128)S(1)} %get-tuple-element.214, f32[2,128]{1,0:T(2,128)S(1)} %get-tuple-element.216, ...), channel_id=1, replica_groups=mesh['dp'=32,'tensor'=4] {'dp','tensor'}, use_global_device_ids=true, to_apply=%region_36.37 | all-reduce | flops 4608 | bytes 36864 | tf_op jit(solution)/shard_map/psum | solution.py:426
  (387 shorter events, 186.3 us)
Async XLA Ops:
  7.2 180.6 %all-gather.33.cloned.1.call-start = ((), (), s32[]{:S(2)}) async-start(), calls=%async_computation.22 | async-start | bytes 1310720 | tf_op jit(solution)/shard_map/all_gather | solution.py:144
  10.9 181.4 %all-gather.49.cloned.1.call-start = ((), (), s32[]{:S(2)}) async-start(), calls=%async_computation.52 | async-start | bytes 1081344 | tf_op jit(solution)/shard_map/all_gather | solution.py:194
  12.4 328.1 %all-gather.51.cloned.1.call-start = ((), (), s32[]{:S(2)}) async-start(), calls=%async_computation.53 | async-start | bytes 1081344 | tf_op jit(solution)/shard_map/all_gather | solution.py:197
  13.9 361.5 %reduce-scatter.23.cloned.1.call-start = ((), (), s32[]{:S(2)}) async-start(), calls=%async_computation.23 | async-start | bytes 1310720 | tf_op jit(solution)/shard_map/reduce_scatter | solution.py:152
  19.3 175.8 %copy-start.18 = (pred[512,512]{0,1:T(8,128)(4,1)}, pred[512,512]{0,1:T(8,128)(4,1)S(1)}, u32[]{:S(2)}) copy-start(pred[512,512]{0,1:T(8,128)(4,1)S(1)} %fusion.104) | copy-start | bytes 786436
  343.6 185.9 %all-gather.53.cloned.1.call-start = ((), (), s32[]{:S(2)}) async-start(), calls=%async_computation.54 | async-start | bytes 1622016 | tf_op jit(solution)/shard_map/all_gather | solution.py:198
  344.3 208.1 %all-gather.35.cloned.1.call-start = ((), (), s32[]{:S(2)}) async-start(), calls=%async_computation.24 | async-start | bytes 1310720 | tf_op jit(solution)/shard_map/all_gather | solution.py:144
  376.5 179.8 %copy-start.65 = (f32[128]{0:T(128)}, f32[128]{0:T(128)S(1)}, u32[]{:S(2)}) copy-start(f32[128]{0:T(128)S(1)} %multiply_reduce_fusion.13) | copy-start | bytes 1540
  378.3 328.2 %all-gather.55.cloned.1.call-start = ((), (), s32[]{:S(2)}) async-start(), calls=%async_computation.55 | async-start | bytes 1622016 | tf_op jit(solution)/shard_map/all_gather | solution.py:199
  379.1 482.1 %all-gather.57.cloned.1.call-start = ((), (), s32[]{:S(2)}) async-start(), calls=%async_computation.56 | async-start | bytes 1622016 | tf_op jit(solution)/shard_map/all_gather | solution.py:200
  379.8 516.9 %reduce-scatter.25.cloned.1.call-start = ((), (), s32[]{:S(2)}) async-start(), calls=%async_computation.25 | async-start | bytes 1310720 | tf_op jit(solution)/shard_map/reduce_scatter | solution.py:152
  552.4 154.1 %copy-start.73 = (bf16[512,1024]{1,0:T(8,128)(2,1)S(1)}, bf16[512,1024]{1,0:T(8,128)(2,1)}, u32[]{:S(2)}) copy-start(bf16[512,1024]{1,0:T(8,128)(2,1)} %all-gather.35.cloned.1.call-done) | copy-start | bytes 3145732
  864.9 202.3 %all-gather.37.cloned.1.call-start = ((), (), s32[]{:S(2)}) async-start(), calls=%async_computation.26 | async-start | bytes 1310720 | tf_op jit(solution)/shard_map/all_gather | solution.py:144
  897.9 171.1 %copy-start.67 = (f32[128]{0:T(128)}, f32[128]{0:T(128)S(1)}, u32[]{:S(2)}) copy-start(f32[128]{0:T(128)S(1)} %get-tuple-element.144) | copy-start | bytes 1540
  898.8 173.6 %all-gather.59.cloned.1.call-start = ((), (), s32[]{:S(2)}) async-start(), calls=%async_computation.57 | async-start | bytes 1081344 | tf_op jit(solution)/shard_map/all_gather | solution.py:194
  899.5 325.5 %all-gather.61.cloned.1.call-start = ((), (), s32[]{:S(2)}) async-start(), calls=%async_computation.58 | async-start | bytes 1081344 | tf_op jit(solution)/shard_map/all_gather | solution.py:197
  900.1 359.9 %reduce-scatter.27.cloned.1.call-start = ((), (), s32[]{:S(2)}) async-start(), calls=%async_computation.27 | async-start | bytes 1310720 | tf_op jit(solution)/shard_map/reduce_scatter | solution.py:152
  1228.2 185.9 %all-gather.65.cloned.1.call-start = ((), (), s32[]{:S(2)}) async-start(), calls=%async_computation.60 | async-start | bytes 1622016 | tf_op jit(solution)/shard_map/all_gather | solution.py:199
  1228.7 207.6 %all-gather.39.cloned.1.call-start = ((), (), s32[]{:S(2)}) async-start(), calls=%async_computation.28 | async-start | bytes 1310720 | tf_op jit(solution)/shard_map/all_gather | solution.py:144
  1262.9 327.5 %all-gather.63.cloned.1.call-start = ((), (), s32[]{:S(2)}) async-start(), calls=%async_computation.59 | async-start | bytes 1622016 | tf_op jit(solution)/shard_map/all_gather | solution.py:198
  1263.5 349.2 %all-gather.41.cloned.1.call-start = ((), (), s32[]{:S(2)}) async-start(), calls=%async_computation.30 | async-start | bytes 1310720 | tf_op jit(solution)/shard_map/all_gather | solution.py:148
  1264.1 502.7 %all-gather.67.cloned.1.call-start = ((), (), s32[]{:S(2)}) async-start(), calls=%async_computation.61 | async-start | bytes 1622016 | tf_op jit(solution)/shard_map/all_gather | solution.py:200
  1264.7 543.1 %reduce-scatter.31.cloned.1.call-start = ((), (), s32[]{:S(2)}) async-start(), calls=%async_computation.31 | async-start | bytes 1310720 | tf_op jit(solution)/shard_map/reduce_scatter | solution.py:161
  1775.8 55.5 %all-gather.43.cloned.1.call-start = ((), (), s32[]{:S(2)}) async-start(), calls=%async_computation.32 | async-start | bytes 1310720 | tf_op jit(solution)/shard_map/all_gather | solution.py:148
  1811.0 85.6 %reduce-scatter.33.cloned.1.call-start = ((), (), s32[]{:S(2)}) async-start(), calls=%async_computation.33 | async-start | bytes 1310720 | tf_op jit(solution)/shard_map/reduce_scatter | solution.py:161
  1865.3 65.5 %reduce-scatter.29.cloned.1.call-start = ((), (), s32[]{:S(2)}) async-start(), calls=%async_computation.29 | async-start | bytes 1310720 | tf_op jit(solution)/shard_map/reduce_scatter | solution.py:152
  1869.1 84.3 %all-gather.45.cloned.1.call-start = ((), (), s32[]{:S(2)}) async-start(), calls=%async_computation.34 | async-start | bytes 1310720 | tf_op jit(solution)/shard_map/all_gather | solution.py:148
  1933.1 59.9 %reduce-scatter.35.cloned.1.call-start = ((), (), s32[]{:S(2)}) async-start(), calls=%async_computation.35 | async-start | bytes 1310720 | tf_op jit(solution)/shard_map/reduce_scatter | solution.py:161
  1961.6 58.0 %all-gather.47.cloned.1.call-start = ((), (), s32[]{:S(2)}) async-start(), calls=%async_computation.36 | async-start | bytes 1310720 | tf_op jit(solution)/shard_map/all_gather | solution.py:148
  1996.1 184.2 %reduce-scatter.65.cloned.1.call-start = ((), (), s32[]{:S(2)}) async-start(), calls=%async_computation.51 | async-start | bytes 1622016 | tf_op jit(solution)/shard_map/reduce_scatter | solution.py:396
  1999.9 341.1 %reduce-scatter.63.cloned.1.call-start = ((), (), s32[]{:S(2)}) async-start(), calls=%async_computation.50 | async-start | bytes 1622016 | tf_op jit(solution)/shard_map/reduce_scatter | solution.py:396
  2003.4 498.8 %reduce-scatter.61.cloned.1.call-start = ((), (), s32[]{:S(2)}) async-start(), calls=%async_computation.49 | async-start | bytes 1622016 | tf_op jit(solution)/shard_map/reduce_scatter | solution.py:393
  2007.2 655.6 %reduce-scatter.59.cloned.1.call-start = ((), (), s32[]{:S(2)}) async-start(), calls=%async_computation.48 | async-start | bytes 1622016 | tf_op jit(solution)/shard_map/reduce_scatter | solution.py:393
  2010.6 813.1 %reduce-scatter.57.cloned.1.call-start = ((), (), s32[]{:S(2)}) async-start(), calls=%async_computation.47 | async-start | bytes 1622016 | tf_op jit(solution)/shard_map/reduce_scatter | solution.py:390
  2014.3 969.8 %reduce-scatter.55.cloned.1.call-start = ((), (), s32[]{:S(2)}) async-start(), calls=%async_computation.46 | async-start | bytes 1622016 | tf_op jit(solution)/shard_map/reduce_scatter | solution.py:390
  2018.1 1124.6 %reduce-scatter.49.cloned.1.call-start = ((), (), s32[]{:S(2)}) async-start(), calls=%async_computation.43 | async-start | bytes 540672 | tf_op jit(solution)/shard_map/reduce_scatter | solution.py:384
  2019.5 1281.5 %reduce-scatter.47.cloned.1.call-start = ((), (), s32[]{:S(2)}) async-start(), calls=%async_computation.42 | async-start | bytes 540672 | tf_op jit(solution)/shard_map/reduce_scatter | solution.py:384
  2027.2 1432.4 %reduce-scatter.45.cloned.1.call-start = ((), (), s32[]{:S(2)}) async-start(), calls=%async_computation.41 | async-start | bytes 540672 | tf_op jit(solution)/shard_map/reduce_scatter | solution.py:381
  2030.0 1588.1 %reduce-scatter.43.cloned.1.call-start = ((), (), s32[]{:S(2)}) async-start(), calls=%async_computation.40 | async-start | bytes 540672 | tf_op jit(solution)/shard_map/reduce_scatter | solution.py:381
  2047.7 1730.0 %reduce-scatter.53.cloned.1.call-start = ((), (), s32[]{:S(2)}) async-start(), calls=%async_computation.45 | async-start | bytes 1081344 | tf_op jit(solution)/shard_map/reduce_scatter | solution.py:387
  2051.0 1885.9 %reduce-scatter.51.cloned.1.call-start = ((), (), s32[]{:S(2)}) async-start(), calls=%async_computation.44 | async-start | bytes 1081344 | tf_op jit(solution)/shard_map/reduce_scatter | solution.py:387
  2064.4 1902.7 %reduce-scatter.37.cloned.1.call-start = ((), (), s32[]{:S(2)}) async-start(), calls=%async_computation.37 | async-start | bytes 1310720 | tf_op jit(solution)/shard_map/reduce_scatter | solution.py:161
  2071.2 2058.4 %reduce-scatter.41.cloned.1.call-start = ((), (), s32[]{:S(2)}) async-start(), calls=%async_computation.39 | async-start | bytes 1081344 | tf_op jit(solution)/shard_map/reduce_scatter | solution.py:378
  2073.1 2215.9 %reduce-scatter.39.cloned.1.call-start = ((), (), s32[]{:S(2)}) async-start(), calls=%async_computation.38 | async-start | bytes 1081344 | tf_op jit(solution)/shard_map/reduce_scatter | solution.py:378
  2076.2 1892.1 %copy-start.64 = (f32[128]{0:T(128)S(1)}, f32[128]{0:T(128)}, u32[]{:S(2)}) copy-start(f32[128]{0:T(128)} %copy-done.63) | copy-start | bytes 1540
  2076.2 2277.3 %copy-start.16 = (bf16[128,1024]{1,0:T(8,128)(2,1)S(1)}, bf16[128,1024]{1,0:T(8,128)(2,1)}, u32[]{:S(2)}) copy-start(bf16[128,1024]{1,0:T(8,128)(2,1)} %reduce-scatter.23.cloned.1.call-done) | copy-start | bytes 786436
  2076.2 2277.3 %copy-start.25 = (f32[128,1024]{1,0:T(8,128)S(1)}, f32[128,1024]{1,0:T(8,128)}, u32[]{:S(2)}) copy-start(f32[128,1024]{1,0:T(8,128)} %copy-done.24) | copy-start | bytes 1572868
  2076.2 2277.3 %copy-start.35 = (bf16[128,1024]{1,0:T(8,128)(2,1)S(1)}, bf16[128,1024]{1,0:T(8,128)(2,1)}, u32[]{:S(2)}) copy-start(bf16[128,1024]{1,0:T(8,128)(2,1)} %reduce-scatter.35.cloned.1.call-done) | copy-start | bytes 786436
  (75 other events, 963.9 us)
Sparse Core Ops, SparseCore 0:
  11.0 23.1 all-gather.32
  36.5 150.6 all-gather.48
  189.4 151.0 all-gather.50
  343.7 31.6 reduce-scatter.22
  377.6 151.8 all-gather.52
  531.6 20.6 all-gather.34
  554.7 151.7 all-gather.54
  708.8 152.3 all-gather.56
  865.0 31.7 reduce-scatter.24
  898.9 20.5 all-gather.36
  921.7 150.5 all-gather.58
  1073.9 151.1 all-gather.60
  1228.3 31.6 reduce-scatter.26
  1262.2 151.7 all-gather.64
  1415.6 20.6 all-gather.38
  1438.5 151.7 all-gather.62
  1592.0 20.6 all-gather.40
  1614.9 151.7 all-gather.66
  1776.0 31.7 reduce-scatter.30
  1811.2 20.1 all-gather.42
  1865.4 31.2 reduce-scatter.32
  1899.5 31.2 reduce-scatter.28
  1933.2 20.1 all-gather.44
  1961.8 31.2 reduce-scatter.34
  1996.2 20.1 all-gather.46
  2018.8 161.5 reduce-scatter.64
  2182.6 158.4 reduce-scatter.62
  2343.6 158.5 reduce-scatter.60
  2504.5 158.2 reduce-scatter.58
  2665.2 158.4 reduce-scatter.56
  2826.0 158.0 reduce-scatter.54
  2986.6 156.1 reduce-scatter.48
  3144.9 156.0 reduce-scatter.46
  3303.5 156.0 reduce-scatter.44
  3462.0 156.0 reduce-scatter.42
  3620.4 157.2 reduce-scatter.52
  3779.9 156.9 reduce-scatter.50
  3939.7 27.3 reduce-scatter.36
  3969.2 160.3 reduce-scatter.40
  4132.1 156.8 reduce-scatter.38
where the time goes:
time: 4370 us; the launch traced here: 4360 us
  waiting for transfers between devices  3720 us (85%)
  blocking collectives  394 us (9%)
  matrix products  154 us (4%)
  other arithmetic  55.7 us (1%)
    reduce_scatter x2, waiting for transfers between devices, body(): lax.psum_scatter(q_part.astype(jnp.bfloat16), 'dp', scatter_dimension=0,...  321 us
    reduce_scatter x2, waiting for transfers between devices, body(): lax.psum_scatter(up_part.astype(jnp.bfloat16), 'dp', scatter_dimension=0,...  320 us
    reduce_scatter x2, waiting for transfers between devices, body(): lax.psum_scatter(gate_part.astype(jnp.bfloat16), 'dp', scatter_dimension=...  320 us
    reduce_scatter x2, waiting for transfers between devices, body(): lax.psum_scatter(o_part.astype(jnp.bfloat16), 'dp', scatter_dimension=1,...  317 us
    reduce_scatter x2, waiting for transfers between devices, body(): lax.psum_scatter(k_part.astype(jnp.bfloat16), 'dp', scatter_dimension=0,...  316 us
    reduce_scatter x2, waiting for transfers between devices, body(): lax.psum_scatter(v_part.astype(jnp.bfloat16), 'dp', scatter_dimension=0,...  315 us
    all_gather x2, waiting for transfers between devices, body(): lax.all_gather(down_weight[decoder_layer_index], 'dp', axis=1, tiled=True)  304 us
    all_gather x2, waiting for transfers between devices, body(): lax.all_gather(gate_weight[decoder_layer_index], 'dp', axis=0, tiled=True)  300 us
  transfers between devices with their start and end apart: 40, of which 36 were waited for; matrix products, arithmetic and copies ran while one was open for 3% of the time, Pallas kernels for 0%

commit v1 on v0

--- a/solution.py
+++ b/solution.py
@@ -140,30 +140,66 @@
     return (grad_query.reshape(query_rotated.shape), sums[0], sums[1])
 
 
+def core_pairs():
+    return [(index, index ^ 1) for index in range(4)]
+
+
+def chip_pairs():
+    return [(index, index ^ 2) for index in range(4)]
+
+
+def dp_shift(stage, step):
+    pairs = []
+    for z in range(4):
+        for x in range(2):
+            for y in range(4):
+                target = {
+                    "y": (z, x, (y + step) % 4),
+                    "x": (z, (x + step) % 2, y),
+                    "z": ((z + step) % 4, x, y),
+                }[stage]
+                pairs.append((z * 8 + x * 4 + y, target[0] * 8 + target[1] * 4 + target[2]))
+    return pairs
+
+
 def gather_rows(row_block):
-    return lax.all_gather(row_block, "tensor", axis=0, tiled=True)
-
-
-def gather_grads(row_block):
-    return lax.all_gather(row_block, "tensor", axis=0, tiled=True)
-
-
-def scatter_rows(term_fn, token_row_count):
-    return lax.psum_scatter(
-        term_fn(jnp.int32(0), lax.axis_size("tensor") * token_row_count).astype(jnp.bfloat16),
-        "tensor",
-        scatter_dimension=0,
-        tiled=True,
-    ).astype(jnp.float32)
-
-
-def scatter_grads(term_fn, token_row_count):
-    return lax.psum_scatter(
-        term_fn(jnp.int32(0), lax.axis_size("tensor") * token_row_count).astype(jnp.bfloat16),
-        "tensor",
-        scatter_dimension=0,
-        tiled=True,
-    ).astype(jnp.float32)
+    index = lax.axis_index("tensor")
+    chip, core = index // 2, index % 2
+    other = lax.ppermute(row_block, "tensor", chip_pairs())
+    pair = jnp.where(chip == 0, jnp.stack([row_block, other]), jnp.stack([other, row_block]))
+    sibling = lax.ppermute(pair, "tensor", core_pairs())
+    both = jnp.where(
+        core == 0, jnp.stack([pair, sibling], axis=1), jnp.stack([sibling, pair], axis=1)
+    )
+    return both.reshape(4 * row_block.shape[0], row_block.shape[1])
+
+
+def scatter_rows(term):
+    index = lax.axis_index("tensor")
+    chip, core = index // 2, index % 2
+    rows, width = term.shape[0] // 4, term.shape[1]
+    blocks = term.reshape(2, 2, rows, width)
+    own = jnp.where(core == 0, blocks[:, 0], blocks[:, 1])
+    away = jnp.where(core == 0, blocks[:, 1], blocks[:, 0]).astype(jnp.bfloat16)
+    summed = own + lax.ppermute(away, "tensor", core_pairs()).astype(jnp.float32)
+    keep = jnp.where(chip == 0, summed[0], summed[1])
+    send = jnp.where(chip == 0, summed[1], summed[0]).astype(jnp.bfloat16)
+    return keep + lax.ppermute(send, "tensor", chip_pairs()).astype(jnp.float32)
+
+
+def sum_everywhere(values):
+    values = values + lax.ppermute(values, "tensor", core_pairs())
+    values = values + lax.ppermute(values, "tensor", chip_pairs())
+    for stage in ("y", "z"):
+        pair = values + lax.ppermute(values, "dp", dp_shift(stage, 1))
+        values = pair + lax.ppermute(pair, "dp", dp_shift(stage, 2))
+    return values + lax.ppermute(values, "dp", dp_shift("x", 1))
+
+
+def pack_weights(layer, q, k, v, o, gate, up, down):
+    return jnp.concatenate(
+        [q[layer], k[layer], v[layer], o[layer].T, gate[layer], up[layer], down[layer].T], axis=1
+    )
 
 
 def body(
@@ -185,21 +221,39 @@
     cosine_table, sine_table = rotary_tables(segment_ids)
     allowed = attention_mask(segment_ids)
     slot_count = segment_ids.shape[0]
-    token_row_count = tokens.shape[0]
     heads_per_group = QUERY_HEADS // KEY_VALUE_HEADS
     residual = tokens.astype(jnp.float32)
     saved_layers = []
+    packed = jnp.concatenate(
+        [
+            pack_weights(
+                layer,
+                q_weight,
+                key_projection,
+                value_projection,
+                o_weight,
+                gate_weight,
+                up_weight,
+                down_weight,
+            )
+            for layer in range(DECODER_LAYERS)
+        ],
+        axis=1,
+    )
+    packed_full = lax.all_gather(packed, "dp", axis=0, tiled=True)
+    layer_width = packed.shape[1] // DECODER_LAYERS
+    weights_by_layer = [
+        jnp.split(
+            packed_full[:, layer * layer_width : (layer + 1) * layer_width],
+            [512, 768, 1024, 1536, 2304, 3072],
+            axis=1,
+        )
+        for layer in range(DECODER_LAYERS)
+    ]
     for decoder_layer_index in range(DECODER_LAYERS):
-        full_weights = (
-            lax.all_gather(q_weight[decoder_layer_index], "dp", axis=0, tiled=True),
-            lax.all_gather(key_projection[decoder_layer_index], "dp", axis=0, tiled=True),
-            lax.all_gather(value_projection[decoder_layer_index], "dp", axis=0, tiled=True),
-            lax.all_gather(o_weight[decoder_layer_index], "dp", axis=1, tiled=True),
-            lax.all_gather(gate_weight[decoder_layer_index], "dp", axis=0, tiled=True),
-            lax.all_gather(up_weight[decoder_layer_index], "dp", axis=0, tiled=True),
-            lax.all_gather(down_weight[decoder_layer_index], "dp", axis=1, tiled=True),
-        )
-        wq_full, wk_full, wv_full, wo_full, wg_full, wu_full, wd_full = full_weights
+        wq_full, wk_full, wv_full, wo_full, wg_full, wu_full, wd_full = weights_by_layer[
+            decoder_layer_index
+        ]
         normed_all = gather_rows(
             rms_scale(residual, attn_norm[decoder_layer_index]).astype(jnp.bfloat16)
         )
@@ -226,10 +280,8 @@
         mixed_heads, log_total = attend_forward(query_rotated, key_rot, value_reduced, allowed)
         mixed_low = mixed_heads.reshape(slot_count, -1).astype(jnp.bfloat16)
 
-        def branch_term(first_row, num_rows):
-            return jnp.dot(mixed_low, wo_full, preferred_element_type=jnp.float32)
-
-        middle = residual + scatter_rows(branch_term, token_row_count)
+        branch = jnp.einsum("sf,df->sd", mixed_low, wo_full, preferred_element_type=jnp.float32)
+        middle = residual + scatter_rows(branch)
         normed_two_all = gather_rows(
             rms_scale(middle, mlp_norm[decoder_layer_index]).astype(jnp.bfloat16)
         )
@@ -237,10 +289,7 @@
         up_pre = jnp.dot(normed_two_all, wu_full, preferred_element_type=jnp.float32)
         product_low = swiglu(gate_pre, up_pre).astype(jnp.bfloat16)
 
-        def feed_term(first_row, num_rows):
-            return jnp.dot(product_low, wd_full, preferred_element_type=jnp.float32)
-
-        kept_weights = None
+        feed = jnp.einsum("sf,df->sd", product_low, wd_full, preferred_element_type=jnp.float32)
         saved_layers.append(
             (
                 residual,
@@ -257,10 +306,9 @@
                 gate_pre,
                 up_pre,
                 product_low,
-                kept_weights,
             )
         )
-        residual = middle + scatter_rows(feed_term, token_row_count)
+        residual = middle + scatter_rows(feed)
     output = residual.astype(jnp.bfloat16)
     grad_rows = cotangent.astype(jnp.float32)
     grads_by_layer = [None] * DECODER_LAYERS
@@ -281,25 +329,17 @@
             gate_pre,
             up_pre,
             product_low,
-            kept_weights,
         ) = saved_layers[decoder_layer_index]
-        full_weights = (
-            lax.all_gather(q_weight[decoder_layer_index], "dp", axis=0, tiled=True),
-            lax.all_gather(key_projection[decoder_layer_index], "dp", axis=0, tiled=True),
-            lax.all_gather(value_projection[decoder_layer_index], "dp", axis=0, tiled=True),
-            lax.all_gather(o_weight[decoder_layer_index], "dp", axis=1, tiled=True),
-            lax.all_gather(gate_weight[decoder_layer_index], "dp", axis=0, tiled=True),
-            lax.all_gather(up_weight[decoder_layer_index], "dp", axis=0, tiled=True),
-            lax.all_gather(down_weight[decoder_layer_index], "dp", axis=1, tiled=True),
-        )
-        wq_full, wk_full, wv_full, wo_full, wg_full, wu_full, wd_full = full_weights
+        wq_full, wk_full, wv_full, wo_full, wg_full, wu_full, wd_full = weights_by_layer[
+            decoder_layer_index
+        ]
         local_kv = key_before_rotary.shape[1]
-        grad_out_all = gather_grads(grad_rows.astype(jnp.bfloat16))
+        grad_out_all = gather_rows(grad_rows.astype(jnp.bfloat16))
         down_part = jnp.einsum(
-            "sf,sd->fd", product_low, grad_out_all, preferred_element_type=jnp.float32
+            "sf,sd->df", product_low, grad_out_all, preferred_element_type=jnp.float32
         )
         grad_product = jnp.einsum(
-            "sd,fd->sf", grad_out_all, wd_full, preferred_element_type=jnp.float32
+            "sd,df->sf", grad_out_all, wd_full, preferred_element_type=jnp.float32
         )
         swiglu_back = jax.vjp(swiglu, gate_pre, up_pre)[1]
         grad_gate, grad_up = swiglu_back(grad_product)
@@ -312,24 +352,22 @@
             "sd,sf->df", normed_two_all, grad_up_low, preferred_element_type=jnp.float32
         )
 
-        def feed_grad_term(first_row, num_rows):
-            first_term = jnp.einsum(
+        first_term = jnp.einsum(
                 "sf,df->sd", grad_gate_low, wg_full, preferred_element_type=jnp.float32
-            )
-            return first_term + jnp.einsum(
+        )
+        second_term = jnp.einsum(
                 "sf,df->sd", grad_up_low, wu_full, preferred_element_type=jnp.float32
-            )
-
-        grad_normed_two = scatter_grads(feed_grad_term, token_row_count)
+        )
+        grad_normed_two = scatter_rows(first_term + second_term)
         norm_back_two = jax.vjp(rms_scale, middle, mlp_norm[decoder_layer_index])[1]
         grad_middle_part, mlp_gain_part = norm_back_two(grad_normed_two)
         grad_middle = grad_rows + grad_middle_part
-        grad_branch_all = gather_grads(grad_middle.astype(jnp.bfloat16))
+        grad_branch_all = gather_rows(grad_middle.astype(jnp.bfloat16))
         o_part = jnp.einsum(
-            "sf,sd->fd", mixed_low, grad_branch_all, preferred_element_type=jnp.float32
+            "sf,sd->df", mixed_low, grad_branch_all, preferred_element_type=jnp.float32
         )
         grad_mixed = jnp.einsum(
-            "sd,fd->sf", grad_branch_all, wo_full, preferred_element_type=jnp.float32
+            "sd,df->sf", grad_branch_all, wo_full, preferred_element_type=jnp.float32
         )
         grad_mixed = grad_mixed.astype(jnp.bfloat16).reshape(
             slot_count, local_kv, heads_per_group, HEAD_SIZE
@@ -358,44 +396,41 @@
             "sd,sf->df", normed_all, grad_value_low, preferred_element_type=jnp.float32
         )
 
-        def attend_grad_term(first_row, num_rows):
-            query_term = jnp.einsum(
-                "sf,df->sd", grad_query_low, wq_full, preferred_element_type=jnp.float32
-            )
-            key_term = jnp.einsum(
-                "sf,df->sd", grad_key_low, wk_full, preferred_element_type=jnp.float32
-            )
-            value_term = jnp.einsum(
-                "sf,df->sd", grad_value_low, wv_full, preferred_element_type=jnp.float32
-            )
-            return query_term + key_term + value_term
-
-        grad_normed = scatter_grads(attend_grad_term, token_row_count)
+        query_term = jnp.einsum(
+            "sf,df->sd", grad_query_low, wq_full, preferred_element_type=jnp.float32
+        )
+        key_term = jnp.einsum(
+            "sf,df->sd", grad_key_low, wk_full, preferred_element_type=jnp.float32
+        )
+        value_term = jnp.einsum(
+            "sf,df->sd", grad_value_low, wv_full, preferred_element_type=jnp.float32
+        )
+
+        grad_normed = scatter_rows(query_term + key_term + value_term)
         norm_back_one = jax.vjp(rms_scale, residual_in, attn_norm[decoder_layer_index])[1]
         grad_in_part, attn_gain_part = norm_back_one(grad_normed)
         grad_rows = grad_middle + grad_in_part
+        grad_packed = jnp.concatenate(
+            [
+                part.astype(jnp.bfloat16)
+                for part in (q_part, k_part, v_part, o_part, gate_part, up_part, down_part)
+            ],
+            axis=1,
+        )
+        grad_rows_own = lax.psum_scatter(
+            grad_packed, "dp", scatter_dimension=0, tiled=True
+        ).astype(jnp.float32)
+        q_own, k_own, v_own, o_own, gate_own, up_own, down_own = jnp.split(
+            grad_rows_own, [512, 768, 1024, 1536, 2304, 3072], axis=1
+        )
         grads_by_layer[decoder_layer_index] = (
-            lax.psum_scatter(
-                q_part.astype(jnp.bfloat16), "dp", scatter_dimension=0, tiled=True
-            ).astype(jnp.float32),
-            lax.psum_scatter(
-                k_part.astype(jnp.bfloat16), "dp", scatter_dimension=0, tiled=True
-            ).astype(jnp.float32),
-            lax.psum_scatter(
-                v_part.astype(jnp.bfloat16), "dp", scatter_dimension=0, tiled=True
-            ).astype(jnp.float32),
-            lax.psum_scatter(
-                o_part.astype(jnp.bfloat16), "dp", scatter_dimension=1, tiled=True
-            ).astype(jnp.float32),
-            lax.psum_scatter(
-                gate_part.astype(jnp.bfloat16), "dp", scatter_dimension=0, tiled=True
-            ).astype(jnp.float32),
-            lax.psum_scatter(
-                up_part.astype(jnp.bfloat16), "dp", scatter_dimension=0, tiled=True
-            ).astype(jnp.float32),
-            lax.psum_scatter(
-                down_part.astype(jnp.bfloat16), "dp", scatter_dimension=1, tiled=True
-            ).astype(jnp.float32),
+            q_own,
+            k_own,
+            v_own,
+            o_own.T,
+            gate_own,
+            up_own,
+            down_own.T,
         )
         gains_by_layer[decoder_layer_index] = (
             attn_gain_part,
@@ -423,8 +458,9 @@
         for member in range(4)
     ]
     attn_gain_stack, q_gain_stack, k_gain_stack, mlp_gain_stack = gain_stack
-    attn_gain_sum, q_gain_sum, k_gain_sum, mlp_gain_sum = lax.psum(
-        (attn_gain_stack, q_gain_stack, k_gain_stack, mlp_gain_stack), ("dp", "tensor")
+    gain_sums = sum_everywhere(jnp.concatenate(gain_stack, axis=1))
+    attn_gain_sum, q_gain_sum, k_gain_sum, mlp_gain_sum = jnp.split(
+        gain_sums, [1024, 1152, 1280], axis=1
     )
     return (
         output,

time: 4370 us -> 812 us (0.19)
  waiting for transfers between devices: 3720 us -> 502 us
  blocking collectives: 394 us -> 0 us
    reduce_scatter x22 -> x0, waiting for transfers between devices: 2420 us -> none  [the longest x2 321 us: body(): lax.psum_scatter(q_part.astype(jnp.bfloat16), 'dp', scatter_dimension=0,...]
    all_gather x18 -> x1, waiting for transfers between devices: 1290 us -> 173 us  [body(): packed_full = lax.all_gather(packed, 'dp', axis=0, tiled=True)]
    all_gather x4 -> x0, blocking collectives: 331 us -> none  [the longest x2 174 us: body(): lax.all_gather(value_projection[decoder_layer_index], 'dp', axis=0, tiled...]
    ppermute x0 -> x39, waiting for transfers between devices: none -> 169 us  [the longest x8 67.5 us: scatter_rows(): return keep + lax.ppermute(send, 'tensor', chip_pairs()).astype(jnp.float32)]
    unnamed x40 -> x5, waiting for transfers between devices: 3.91 us -> 160 us
    psum x1 -> x0, blocking collectives: 63 us -> none  [body(): lax.psum((attn_gain_stack, q_gain_stack, k_gain_stack, mlp_gain_stack), (...]
    ppermute x0 -> x39, starting transfers between devices: none -> 46 us  [the longest x8 22.3 us: gather_rows(): other = lax.ppermute(row_block, 'tensor', chip_pairs())]
  transfers between devices with their start and end apart: 40 -> 42, of which waited for: 36 -> 35; matrix products, arithmetic and copies ran while one was open for 3% -> 13% of each run, Pallas kernels for 0% -> 0%
where the time goes in v1:
time: 812 us; the launch traced here: 802 us
  waiting for transfers between devices  502 us (62%)
  matrix products  135 us (17%)
  local copies, waits for them, and re-layouts  60.4 us (7%)
  starting transfers between devices  46.2 us (6%)
  other arithmetic  41.7 us (5%)
  between operations  16.2 us (2%)
    all_gather x1, waiting for transfers between devices, body(): packed_full = lax.all_gather(packed, 'dp', axis=0, tiled=True)  173 us
    unnamed x5, waiting for transfers between devices  160 us
    ppermute x8, waiting for transfers between devices, scatter_rows(): return keep + lax.ppermute(send, 'tensor', chip_pairs()).astype(jnp.float32)  67.5 us
    ppermute x8, waiting for transfers between devices, gather_rows(): other = lax.ppermute(row_block, 'tensor', chip_pairs())  54.8 us
    unnamed x189, local copies, waits for them, and re-layouts  40.3 us
    ppermute x8, starting transfers between devices, gather_rows(): other = lax.ppermute(row_block, 'tensor', chip_pairs())  22.3 us
    ppermute x8, starting transfers between devices, scatter_rows(): return keep + lax.ppermute(send, 'tensor', chip_pairs()).astype(jnp.float32)  18.6 us
    dot_general x2, matrix products, one_step(): jnp.einsum('hgqk,qhgd->khd', grad_score, query_block, preferred_element_t...  18.1 us
  transfers between devices with their start and end apart: 42, of which 35 were waited for; matrix products, arithmetic and copies ran while one was open for 13% of the time, Pallas kernels for 0%

profile of v1, /device:TPU:0, one launch (start us, length us, event | category | flops | bytes accessed | tf_op | source)
XLA Modules:
  0.0 802.0 jit_solution(10525011615682553079)
XLA Ops:
  21.8 3.2 collective-permute-start
  26.4 3.3 subtract_convert_fusion
  35.7 173.3 %all-gather.2.cloned.1.call-done = bf16[1024,7680]{1,0:T(8,128)(2,1)} async-done(((bf16[32,7680]{1,0:T(8,128)(2,1)}), bf16[1024,7680]{1,0:T(8,128)(2,1)}) %all-gather.2.cloned.1.call-update) | async-done | bytes 15728656 | tf_op jit(solution)/shard_map/all_gather | solution.py:243
  212.7 2.7 slice_bitcast_fusion.12
  231.5 7.5 collective-permute-done.3
  241.9 6.5 collective-permute-done.4
  250.9 2.8 fusion.66
  253.7 4.1 multiply_convert_fusion.3
  257.8 2.7 fusion.59
  265.5 7.5 collective-permute-done.7
  275.9 6.5 collective-permute-done.8
  302.9 2.6 collective-permute-start.16
  307.3 6.5 collective-permute-done.16
  313.9 4.6 collective-permute-done.11
  321.5 6.5 collective-permute-done.12
  330.3 2.8 fusion.51
  335.5 3.8 multiply_convert_fusion.1
  339.3 3.0 fusion.53
  349.6 7.5 collective-permute-done.19
  360.8 6.7 collective-permute-done.20
  373.3 2.8 fusion.204
  377.6 9.1 %broadcast_multiply_fusion.1 = (f32[512,2,128]{0,2,1:T(8,128)}, f32[512,2,128]{0,2,1:T(8,128)}) fusion(f32[512,128]{0,1:T(8,128)S(1)} %get-tuple-element.221, bf16[512,2,2,128]{0,3,2,1:T(8,128)(2,1)} %bitcast.688, f32[2,512,512,2]{2,1,3,0:T(8,128)} %fusion.204, f32[2,2,512,512]{2,3,1,0:T(8,128)} %copy-done.2, f32[2,2,512]{2,1,0:T(2,128)S(1)} %log_add_fusion.1), kind=kOutput, calls=%fused_computation.350 | convolution fusion | flops 275909120 | bytes 10231808 | tf_op jit(solution)/shard_map/while/body/eval_jaxpr/hgqk,qhgd->khd/dot_general | solution.py:124
  386.7 9.1 %fusion.25 = f32[2,128,2,512]{3,1,2,0:T(8,128)} fusion(bf16[512,2,128,1]{0,2,3,1:T(8,128)(2,1)} %copy-done.53, f32[2,512,512,2]{2,1,3,0:T(8,128)} %fusion.204, f32[2,2,512,512]{2,3,1,0:T(8,128)} %copy-done.2, f32[2,2,512]{2,1,0:T(2,128)S(1)} %log_add_fusion.1), kind=kOutput, calls=%fused_computation.39 | convolution fusion | flops 275778048 | bytes 9707520 | tf_op jit(solution)/shard_map/while/body/eval_jaxpr/hgqk,khd->qhgd/dot_general | solution.py:121
  414.0 10.4 %copy.243 = bf16[1024,3840]{1,0:T(8,128)(2,1)} copy(bf16[1024,3840]{0,1:T(8,128)(2,1)} %fusion.33) | data formatting | bytes 15728640
  430.2 2.5 fusion.48
  437.8 8.8 %collective-permute-done.23 = bf16[128,1024]{1,0:T(8,128)(2,1)S(1)} collective-permute-done((bf16[128,1024]{1,0:T(8,128)(2,1)S(1)}, bf16[128,1024]{1,0:T(8,128)(2,1)S(1)}, u32[]{:S(2)}, u32[]{:S(2)}) %collective-permute-start.23) | collective-permute-done | bytes 262176 | tf_op jit(solution)/shard_map/ppermute | solution.py:187
  446.8 8.3 %collective-permute-done.15 = bf16[128,1024]{1,0:T(8,128)(2,1)S(1)} collective-permute-done((bf16[128,1024]{1,0:T(8,128)(2,1)S(1)}, bf16[128,1024]{1,0:T(8,128)(2,1)S(1)}, u32[]{:S(2)}, u32[]{:S(2)}) %collective-permute-start.15) | collective-permute-done | bytes 262176 | tf_op jit(solution)/shard_map/ppermute | solution.py:187
  456.1 3.6 collective-permute-start.24
  459.7 10.5 %collective-permute-done.24 = bf16[128,1024]{1,0:T(8,128)(2,1)S(1)} collective-permute-done((bf16[128,1024]{1,0:T(8,128)(2,1)S(1)}, bf16[128,1024]{1,0:T(8,128)(2,1)S(1)}, u32[]{:S(2)}, u32[]{:S(2)}) %collective-permute-start.24) | collective-permute-done | bytes 262176 | tf_op jit(solution)/shard_map/ppermute | solution.py:168
  472.6 3.2 multiply_convert_fusion
  475.9 3.0 fusion.64
  483.8 3.3 collective-permute-start.27
  487.1 11.7 %collective-permute-done.27 = bf16[128,1024]{1,0:T(8,128)(2,1)S(1)} collective-permute-done((bf16[128,1024]{1,0:T(8,128)(2,1)S(1)}, bf16[128,1024]{1,0:T(8,128)(2,1)S(1)}, u32[]{:S(2)}, u32[]{:S(2)}) %collective-permute-start.27) | collective-permute-done | bytes 262176 | tf_op jit(solution)/shard_map/ppermute | solution.py:187
  500.0 3.1 collective-permute-start.28
  503.1 11.6 %collective-permute-done.28 = bf16[128,1024]{1,0:T(8,128)(2,1)S(1)} collective-permute-done((bf16[128,1024]{1,0:T(8,128)(2,1)S(1)}, bf16[128,1024]{1,0:T(8,128)(2,1)S(1)}, u32[]{:S(2)}, u32[]{:S(2)}) %collective-permute-start.28) | collective-permute-done | bytes 262176 | tf_op jit(solution)/shard_map/ppermute | solution.py:168
  520.4 2.7 fusion.205
  523.2 9.0 %broadcast_multiply_fusion = (f32[512,2,128]{0,2,1:T(8,128)S(1)}, f32[512,2,128]{0,2,1:T(8,128)}) fusion(f32[512,128]{0,1:T(8,128)S(1)} %get-tuple-element.221, bf16[512,2,2,128]{0,3,2,1:T(8,128)(2,1)S(1)} %bitcast.686, f32[2,512,512,2]{2,1,3,0:T(8,128)} %fusion.205, f32[2,2,512,512]{2,3,1,0:T(8,128)} %copy-done, f32[2,2,512]{2,1,0:T(2,128)S(1)} %log_add_fusion), kind=kOutput, calls=%fused_computation.349 | convolution fusion | flops 275909120 | bytes 10231808 | tf_op jit(solution)/shard_map/while/body/eval_jaxpr/hgqk,qhgd->khd/dot_general | solution.py:124
  534.2 8.1 %fusion.19 = f32[2,128,2,512]{3,1,2,0:T(8,128)S(1)} fusion(bf16[512,2,128,1]{0,2,3,1:T(8,128)(2,1)} %copy-done.52, f32[2,512,512,2]{2,1,3,0:T(8,128)} %fusion.205, f32[2,2,512,512]{2,3,1,0:T(8,128)} %copy-done, f32[2,2,512]{2,1,0:T(2,128)S(1)} %log_add_fusion), kind=kOutput, calls=%fused_computation.32 | convolution fusion | flops 275778048 | bytes 9707520 | tf_op jit(solution)/shard_map/while/body/eval_jaxpr/hgqk,khd->qhgd/dot_general | solution.py:121
  557.5 10.6 %copy.241 = bf16[1024,3840]{1,0:T(8,128)(2,1)} copy(bf16[1024,3840]{0,1:T(8,128)(2,1)} %fusion.30) | data formatting | bytes 15728640
  575.7 2.9 collective-permute-start.31
  578.5 11.7 %collective-permute-done.31 = bf16[128,1024]{1,0:T(8,128)(2,1)S(1)} collective-permute-done((bf16[128,1024]{1,0:T(8,128)(2,1)S(1)}, bf16[128,1024]{1,0:T(8,128)(2,1)S(1)}, u32[]{:S(2)}, u32[]{:S(2)}) %collective-permute-start.31) | collective-permute-done | bytes 262176 | tf_op jit(solution)/shard_map/ppermute | solution.py:187
  592.7 4.5 collective-permute-done.33
  597.2 5.0 collective-permute-done.34
  602.3 5.3 collective-permute-done.35
  607.7 5.0 collective-permute-done.36
  612.8 5.2 collective-permute-done.37
  619.1 2.9 collective-permute-done.38
  629.2 159.8 %reduce-scatter.7.cloned.1.call-done = bf16[32,3840]{1,0:T(8,128)(2,1)} async-done(((bf16[1024,3840]{1,0:T(8,128)(2,1)}), bf16[32,3840]{1,0:T(8,128)(2,1)}) %reduce-scatter.7.cloned.1.call-update) | async-done | bytes 245776
  (464 shorter events, 188.3 us)
Async XLA Ops:
  7.2 27.3 %copy-start.6 = (bf16[128,1024]{1,0:T(8,128)(2,1)S(1)}, bf16[128,1024]{1,0:T(8,128)(2,1)}, u32[]{:S(2)}) copy-start(bf16[128,1024]{1,0:T(8,128)(2,1)} %param.14) | copy-start | bytes 786436
  7.2 26.3 %copy-start.72 = (f32[2,128]{1,0:T(2,128)S(1)}, f32[2,128]{1,0:T(2,128)}, u32[]{:S(2)}) copy-start(f32[2,128]{1,0:T(2,128)} %param.23) | copy-start | bytes 3076
  7.2 201.8 %all-gather.2.cloned.1.call-start = ((), (), s32[]{:S(2)}) async-start(), calls=%async_computation.2 | async-start | bytes 16220160 | tf_op jit(solution)/shard_map/all_gather | solution.py:243
  18.8 604.4 %reduce-scatter.9.cloned.1.call-start = ((), (), s32[]{:S(2)}) async-start(), calls=%async_computation.4 | async-start | bytes 8110080
  21.8 11.5 %collective-permute-start = (bf16[128,1024]{1,0:T(8,128)(2,1)S(1)}, bf16[128,1024]{1,0:T(8,128)(2,1)S(1)}, u32[]{:S(2)}, u32[]{:S(2)}) collective-permute-start(bf16[128,1024]{1,0:T(8,128)(2,1)S(1)} %fusion.117), channel_id=1, source_target_pairs={{0,2},{1,3},{2,0},{3,1},{4,6},{5,7},{6,4},{7,5},{8,10},{9,11},{10,... | collective-permute-start | bytes 786440 | tf_op jit(solution)/shard_map/ppermute | solution.py:168
  33.4 2.0 collective-permute-start.1
  35.7 185.8 %copy-start.7 = (bf16[2,2,128,1024]{3,2,1,0:T(8,128)(2,1)}, bf16[2,2,128,1024]{3,2,1,0:T(8,128)(2,1)S(1)}, u32[]{:S(2)}) copy-start(bf16[2,2,128,1024]{3,2,1,0:T(8,128)(2,1)S(1)} %copy.133) | copy-start | bytes 3145732
  226.6 2.0 collective-permute-start.2
  229.0 9.9 %collective-permute-start.3 = (bf16[128,1024]{1,0:T(8,128)(2,1)S(1)}, bf16[128,1024]{1,0:T(8,128)(2,1)S(1)}, u32[]{:S(2)}, u32[]{:S(2)}) collective-permute-start(bf16[128,1024]{1,0:T(8,128)(2,1)S(1)} %fusion.157), channel_id=1, source_target_pairs={{0,2},{1,3},{2,0},{3,1},{4,6},{5,7},{6,4},{7,5},{8,10},{9,11},{10,... | collective-permute-start | bytes 786440 | tf_op jit(solution)/shard_map/ppermute | solution.py:187
  239.3 9.1 %collective-permute-start.4 = (bf16[128,1024]{1,0:T(8,128)(2,1)S(1)}, bf16[128,1024]{1,0:T(8,128)(2,1)S(1)}, u32[]{:S(2)}, u32[]{:S(2)}) collective-permute-start(bf16[128,1024]{1,0:T(8,128)(2,1)S(1)} %multiply_convert_fusion.6), channel_id=1, source_target_pairs={{0,2},{1,3},{2,0},{3,1},{4,6},{5,7},{6,4},{7,5},{8,10},{9,11},{10,... | collective-permute-start | bytes 786440 | tf_op jit(solution)/shard_map/ppermute | solution.py:168
  248.5 2.2 collective-permute-start.5
  260.7 23.3 %copy-start.32 = (bf16[256,1024]{0,1:T(8,128)(2,1)S(1)}, bf16[256,1024]{0,1:T(8,128)(2,1)}, u32[]{:S(2)}) copy-start(bf16[256,1024]{0,1:T(8,128)(2,1)} %get-tuple-element.182) | copy-start | bytes 1572868
  260.7 2.0 collective-permute-start.6
  263.0 9.9 %collective-permute-start.7 = (bf16[128,1024]{1,0:T(8,128)(2,1)S(1)}, bf16[128,1024]{1,0:T(8,128)(2,1)S(1)}, u32[]{:S(2)}, u32[]{:S(2)}) collective-permute-start(bf16[128,1024]{1,0:T(8,128)(2,1)S(1)} %fusion.158), channel_id=1, source_target_pairs={{0,2},{1,3},{2,0},{3,1},{4,6},{5,7},{6,4},{7,5},{8,10},{9,11},{10,... | collective-permute-start | bytes 786440 | tf_op jit(solution)/shard_map/ppermute | solution.py:187
  273.3 9.1 %collective-permute-start.8 = (bf16[128,1024]{1,0:T(8,128)(2,1)S(1)}, bf16[128,1024]{1,0:T(8,128)(2,1)S(1)}, u32[]{:S(2)}, u32[]{:S(2)}) collective-permute-start(bf16[128,1024]{1,0:T(8,128)(2,1)S(1)} %multiply_convert_fusion.5), channel_id=1, source_target_pairs={{0,2},{1,3},{2,0},{3,1},{4,6},{5,7},{6,4},{7,5},{8,10},{9,11},{10,... | collective-permute-start | bytes 786440 | tf_op jit(solution)/shard_map/ppermute | solution.py:168
  284.0 4.6 collective-permute-start.9
  302.3 3.1 collective-permute-start.10
  302.9 10.9 %collective-permute-start.16 = (bf16[128,1024]{1,0:T(8,128)(2,1)S(1)}, bf16[128,1024]{1,0:T(8,128)(2,1)S(1)}, u32[]{:S(2)}, u32[]{:S(2)}) collective-permute-start(bf16[128,1024]{1,0:T(8,128)(2,1)S(1)} %copy-done.21), channel_id=1, source_target_pairs={{0,2},{1,3},{2,0},{3,1},{4,6},{5,7},{6,4},{7,5},{8,10},{9,11},{10,... | collective-permute-start | bytes 786440 | tf_op jit(solution)/shard_map/ppermute | solution.py:168
  305.8 12.7 %collective-permute-start.11 = (bf16[128,1024]{1,0:T(8,128)(2,1)S(1)}, bf16[128,1024]{1,0:T(8,128)(2,1)S(1)}, u32[]{:S(2)}, u32[]{:S(2)}) collective-permute-start(bf16[128,1024]{1,0:T(8,128)(2,1)S(1)} %fusion.159), channel_id=1, source_target_pairs={{0,2},{1,3},{2,0},{3,1},{4,6},{5,7},{6,4},{7,5},{8,10},{9,11},{10,... | collective-permute-start | bytes 786440 | tf_op jit(solution)/shard_map/ppermute | solution.py:187
  313.8 14.4 %collective-permute-start.17 = (bf16[2,128,1024]{2,1,0:T(8,128)(2,1)S(1)}, bf16[2,128,1024]{2,1,0:T(8,128)(2,1)S(1)}, u32[]{:S(2)}, u32[]{:S(2)}) collective-permute-start(bf16[2,128,1024]{2,1,0:T(8,128)(2,1)S(1)} %maximum_select_fusion.14), channel_id=1, source_target_pairs={{0,1},{1,0},{2,3},{3,2},{4,5},{5,4},{6,7},{7,6},{8,9},{9,8},{10,11... | collective-permute-start | bytes 1572872 | tf_op jit(solution)/shard_map/ppermute | solution.py:170
  318.9 9.1 %collective-permute-start.12 = (bf16[128,1024]{1,0:T(8,128)(2,1)S(1)}, bf16[128,1024]{1,0:T(8,128)(2,1)S(1)}, u32[]{:S(2)}, u32[]{:S(2)}) collective-permute-start(bf16[128,1024]{1,0:T(8,128)(2,1)S(1)} %multiply_convert_fusion.4), channel_id=1, source_target_pairs={{0,2},{1,3},{2,0},{3,1},{4,6},{5,7},{6,4},{7,5},{8,10},{9,11},{10,... | collective-permute-start | bytes 786440 | tf_op jit(solution)/shard_map/ppermute | solution.py:168
  328.1 2.0 collective-permute-start.13
  344.9 2.0 collective-permute-start.18
  347.2 9.9 %collective-permute-start.19 = (bf16[128,1024]{1,0:T(8,128)(2,1)S(1)}, bf16[128,1024]{1,0:T(8,128)(2,1)S(1)}, u32[]{:S(2)}, u32[]{:S(2)}) collective-permute-start(bf16[128,1024]{1,0:T(8,128)(2,1)S(1)} %fusion.161), channel_id=1, source_target_pairs={{0,2},{1,3},{2,0},{3,1},{4,6},{5,7},{6,4},{7,5},{8,10},{9,11},{10,... | collective-permute-start | bytes 786440 | tf_op jit(solution)/shard_map/ppermute | solution.py:187
  358.3 9.1 %collective-permute-start.20 = (bf16[128,1024]{1,0:T(8,128)(2,1)S(1)}, bf16[128,1024]{1,0:T(8,128)(2,1)S(1)}, u32[]{:S(2)}, u32[]{:S(2)}) collective-permute-start(bf16[128,1024]{1,0:T(8,128)(2,1)S(1)} %fusion.185), channel_id=1, source_target_pairs={{0,2},{1,3},{2,0},{3,1},{4,6},{5,7},{6,4},{7,5},{8,10},{9,11},{10,... | collective-permute-start | bytes 786440 | tf_op jit(solution)/shard_map/ppermute | solution.py:168
  367.5 2.4 collective-permute-start.21
  424.4 364.6 %reduce-scatter.7.cloned.1.call-start = ((), (), s32[]{:S(2)}) async-start(), calls=%async_computation.3 | async-start | bytes 8110080
  430.0 3.3 collective-permute-start.22
  432.8 3.2 collective-permute-start.14
  433.7 12.9 %collective-permute-start.23 = (bf16[128,1024]{1,0:T(8,128)(2,1)S(1)}, bf16[128,1024]{1,0:T(8,128)(2,1)S(1)}, u32[]{:S(2)}, u32[]{:S(2)}) collective-permute-start(bf16[128,1024]{1,0:T(8,128)(2,1)S(1)} %fusion.162), channel_id=1, source_target_pairs={{0,2},{1,3},{2,0},{3,1},{4,6},{5,7},{6,4},{7,5},{8,10},{9,11},{10,... | collective-permute-start | bytes 786440 | tf_op jit(solution)/shard_map/ppermute | solution.py:187
  436.4 18.7 %collective-permute-start.15 = (bf16[128,1024]{1,0:T(8,128)(2,1)S(1)}, bf16[128,1024]{1,0:T(8,128)(2,1)S(1)}, u32[]{:S(2)}, u32[]{:S(2)}) collective-permute-start(bf16[128,1024]{1,0:T(8,128)(2,1)S(1)} %fusion.160), channel_id=1, source_target_pairs={{0,2},{1,3},{2,0},{3,1},{4,6},{5,7},{6,4},{7,5},{8,10},{9,11},{10,... | collective-permute-start | bytes 786440 | tf_op jit(solution)/shard_map/ppermute | solution.py:187
  456.1 14.2 %collective-permute-start.24 = (bf16[128,1024]{1,0:T(8,128)(2,1)S(1)}, bf16[128,1024]{1,0:T(8,128)(2,1)S(1)}, u32[]{:S(2)}, u32[]{:S(2)}) collective-permute-start(bf16[128,1024]{1,0:T(8,128)(2,1)S(1)} %get-tuple-element.166), channel_id=1, source_target_pairs={{0,2},{1,3},{2,0},{3,1},{4,6},{5,7},{6,4},{7,5},{8,10},{9,11},{10,... | collective-permute-start | bytes 786440 | tf_op jit(solution)/shard_map/ppermute | solution.py:168
  470.3 2.0 collective-permute-start.25
  481.5 2.0 collective-permute-start.26
  483.8 15.0 %collective-permute-start.27 = (bf16[128,1024]{1,0:T(8,128)(2,1)S(1)}, bf16[128,1024]{1,0:T(8,128)(2,1)S(1)}, u32[]{:S(2)}, u32[]{:S(2)}) collective-permute-start(bf16[128,1024]{1,0:T(8,128)(2,1)S(1)} %fusion.163), channel_id=1, source_target_pairs={{0,2},{1,3},{2,0},{3,1},{4,6},{5,7},{6,4},{7,5},{8,10},{9,11},{10,... | collective-permute-start | bytes 786440 | tf_op jit(solution)/shard_map/ppermute | solution.py:187
  500.0 14.7 %collective-permute-start.28 = (bf16[128,1024]{1,0:T(8,128)(2,1)S(1)}, bf16[128,1024]{1,0:T(8,128)(2,1)S(1)}, u32[]{:S(2)}, u32[]{:S(2)}) collective-permute-start(bf16[128,1024]{1,0:T(8,128)(2,1)S(1)} %get-tuple-element.163), channel_id=1, source_target_pairs={{0,2},{1,3},{2,0},{3,1},{4,6},{5,7},{6,4},{7,5},{8,10},{9,11},{10,... | collective-permute-start | bytes 786440 | tf_op jit(solution)/shard_map/ppermute | solution.py:168
  514.8 2.2 collective-permute-start.29
  573.3 39.5 %copy-start.74 = (f32[128]{0:T(128)S(1)}, f32[128]{0:T(128)}, u32[]{:S(2)}) copy-start(f32[128]{0:T(128)} %copy-done.73) | copy-start | bytes 1540
  573.3 44.8 %copy-start.29 = (f32[128,1024]{1,0:T(8,128)S(1)}, f32[128,1024]{1,0:T(8,128)}, u32[]{:S(2)}) copy-start(f32[128,1024]{1,0:T(8,128)} %get-tuple-element.164) | copy-start | bytes 1572868
  573.4 2.0 collective-permute-start.30
  575.7 14.5 %collective-permute-start.31 = (bf16[128,1024]{1,0:T(8,128)(2,1)S(1)}, bf16[128,1024]{1,0:T(8,128)(2,1)S(1)}, u32[]{:S(2)}, u32[]{:S(2)}) collective-permute-start(bf16[128,1024]{1,0:T(8,128)(2,1)S(1)} %fusion.164), channel_id=1, source_target_pairs={{0,2},{1,3},{2,0},{3,1},{4,6},{5,7},{6,4},{7,5},{8,10},{9,11},{10,... | collective-permute-start | bytes 786440 | tf_op jit(solution)/shard_map/ppermute | solution.py:187
  590.5 1.3 collective-permute-start.32
  591.8 5.3 collective-permute-start.33
  597.2 5.0 collective-permute-start.34
  602.2 5.3 collective-permute-start.35
  607.6 5.0 collective-permute-start.36
  612.6 5.3 collective-permute-start.37
  618.0 4.0 collective-permute-start.38
  (80 other events, 409.4 us)
Sparse Core Ops, SparseCore 0:
  18.9 190.0 all-gather.1
  424.5 182.7 reduce-scatter.8
  610.0 179.0 reduce-scatter.6

commit v2 on v0

v2 whole, which is shorter than its diff:
```python
import math

import jax
import jax.numpy as jnp
from jax import lax
from jax.experimental import pallas as pl
from jax.experimental.pallas import tpu as pltpu
from jax.sharding import PartitionSpec as P

ROPE_BASE = 1000000.0
HEAD = 128
SCALE = 128 ** -0.5
LOG2E = 1.0 / math.log(2.0)
NORM_EPS = 1e-6
NT = (((1,), (1,)), ((), ()))
TN = (((0,), (0,)), ((), ()))
NN = (((1,), (0,)), ((), ()))


def block_offsets():
    core = lax.axis_index("tensor") % 2
    return [
        pl.multiple_of(128 * (block // 2 + 2 * ((block + core) % 2)), 128) for block in range(4)
    ]


def block_mask(block, segment_rows, segment_columns):
    keys = 128 * (block + 1)
    row = lax.broadcasted_iota(jnp.int32, (128, keys), 0) + 128 * block
    column = lax.broadcasted_iota(jnp.int32, (128, keys), 1)
    query_segment = segment_rows[128 * block : 128 * (block + 1), :]
    same = query_segment == segment_columns[:, :keys]
    allowed = same & (column <= row) & (query_segment < 3) | (column == row)
    return allowed.astype(jnp.float32)


def head_norm(pre):
    return lax.rsqrt(jnp.mean(pre * pre, axis=-1, keepdims=True) + NORM_EPS)


def attend_forward_kernel(
    pre_qk, pre_v, q_gain, k_gain, cosine, sine, segment_rows, segment_columns, rotated, mixed, inverse, keys
):
    offsets = block_offsets()
    cos, sin = cosine[...], sine[...]
    for head in range(6):
        lanes = slice(128 * head, 128 * (head + 1))
        value = pre_qk[:, lanes]
        gain = q_gain[...] if head < 4 else k_gain[...]
        normed = value * head_norm(value) * gain
        turned = normed * cos + pltpu.roll(normed, 64, 1) * sin
        rotated[:, lanes] = turned.astype(jnp.bfloat16)
    rotated[:, 768:] = pre_v[...].astype(jnp.bfloat16)
    for block in range(4):
        keys[128 * block : 128 * (block + 1), :] = rotated[pl.ds(offsets[block], 128), 512:]
    lane = lax.broadcasted_iota(jnp.int32, (128, 128), 1)
    for block in range(4):
        count = 128 * (block + 1)
        allowed = block_mask(block, segment_rows, segment_columns)
        allowed = jnp.concatenate([allowed, allowed], axis=0)
        rows = pl.ds(offsets[block], 128)
        totals = jnp.zeros((128, 128), jnp.float32)
        for group in range(2):
            query = jnp.concatenate(
                [rotated[rows, 256 * group : 256 * group + 128], rotated[rows, 256 * group + 128 : 256 * group + 256]],
                axis=0,
            )
            key = keys[:count, 128 * group : 128 * (group + 1)]
            value = keys[:count, 256 + 128 * group : 256 + 128 * (group + 1)]
            score = lax.dot_general(query, key, NT, preferred_element_type=jnp.float32)
            weight = jnp.exp2(score * (SCALE * LOG2E)) * allowed
            inverse_total = 1.0 / jnp.sum(weight, axis=-1, keepdims=True)
            out = lax.dot_general((weight * inverse_total).astype(jnp.bfloat16), value, NN, preferred_element_type=jnp.float32)
            out = out.astype(jnp.bfloat16)
            mixed[rows, 256 * group : 256 * group + 128] = out[:128]
            mixed[rows, 256 * group + 128 : 256 * group + 256] = out[128:]
            totals = jnp.where(lane == 2 * group, inverse_total[:128], totals)
            totals = jnp.where(lane == 2 * group + 1, inverse_total[128:], totals)
        inverse[rows, :] = totals


def attend_forward(pre_qk, pre_v, q_gain, k_gain, cosine, sine, segment_rows, segment_columns):
    return pl.pallas_call(
        attend_forward_kernel,
        out_shape=(
            jax.ShapeDtypeStruct((512, 1024), jnp.bfloat16),
            jax.ShapeDtypeStruct((512, 512), jnp.bfloat16),
            jax.ShapeDtypeStruct((512, 128), jnp.float32),
        ),
        scratch_shapes=[pltpu.VMEM((512, 512), jnp.bfloat16)],
        compiler_params=pltpu.CompilerParams(vmem_limit_bytes=24 * 1024 * 1024),
        cost_estimate=pl.CostEstimate(flops=700_000_000, bytes_accessed=6_000_000, transcendentals=700_000),
        name="attend_forward",
    )(pre_qk, pre_v, q_gain, k_gain, cosine, sine, segment_rows, segment_columns)


def attend_backward_kernel(
    pre_qk, rotated, mixed, inverse, grad_mixed, q_gain, k_gain, cosine, sine, segment_rows, segment_columns,
    grad_qk, grad_v, gain_grads, keys, grad_rotated, grad_keys,
):
    offsets = block_offsets()
    for block in range(4):
        keys[128 * block : 128 * (block + 1), :] = rotated[pl.ds(offsets[block], 128), 512:]
    for block in range(3, -1, -1):
        count = 128 * (block + 1)
        allowed = block_mask(block, segment_rows, segment_columns)
        allowed = jnp.concatenate([allowed, allowed], axis=0)
        rows = pl.ds(offsets[block], 128)
        inverse_block = inverse[rows, :]
        for group in range(2):
            def pair(ref):
                return jnp.concatenate(
                    [ref[rows, 256 * group : 256 * group + 128], ref[rows, 256 * group + 128 : 256 * group + 256]],
                    axis=0,
                )
            query, grad_out = pair(rotated), pair(grad_mixed)
            inner = jnp.sum(grad_out.astype(jnp.float32) * pair(mixed).astype(jnp.float32), axis=-1, keepdims=True)
            key = keys[:count, 128 * group : 128 * (group + 1)]
            value = keys[:count, 256 + 128 * group : 256 + 128 * (group + 1)]
            inverse_total = jnp.concatenate(
                [inverse_block[:, 2 * group : 2 * group + 1], inverse_block[:, 2 * group + 1 : 2 * group + 2]], axis=0
            )
            score = lax.dot_general(query, key, NT, preferred_element_type=jnp.float32)
            weight = jnp.exp2(score * (SCALE * LOG2E)) * allowed * inverse_total
            grad_weight = lax.dot_general(grad_out, value, NT, preferred_element_type=jnp.float32)
            grad_score = (weight * (grad_weight - inner)).astype(jnp.bfloat16)
            low = weight.astype(jnp.bfloat16)
            grad_value = lax.dot_general(low, grad_out, TN, preferred_element_type=jnp.float32)
            grad_key = lax.dot_general(grad_score, query, TN, preferred_element_type=jnp.float32)
            grad_query = lax.dot_general(grad_score, key, NN, preferred_element_type=jnp.float32)
            grad_rotated[rows, 256 * group : 256 * group + 128] = grad_query[:128] * SCALE
            grad_rotated[rows, 256 * group + 128 : 256 * group + 256] = grad_query[128:] * SCALE
            spot, value_spot = slice(128 * group, 128 * (group + 1)), slice(256 + 128 * group, 256 + 128 * (group + 1))
            if block == 3:
                grad_keys[:, spot] = grad_key * SCALE
                grad_keys[:, value_spot] = grad_value
            else:
                grad_keys[:count, spot] += grad_key * SCALE
                grad_keys[:count, value_spot] += grad_value
    for block in range(4):
        grad_rotated[pl.ds(offsets[block], 128), 512:] = grad_keys[128 * block : 128 * (block + 1), :]
    cos, sin = cosine[...], sine[...]
    gain_sums = []
    for head in range(6):
        lanes = slice(128 * head, 128 * (head + 1))
        value = pre_qk[:, lanes]
        gain = q_gain[...] if head < 4 else k_gain[...]
        scale = head_norm(value)
        unit = value * scale
        turned = grad_rotated[:, lanes]
        grad = turned * cos + pltpu.roll(turned * sin, 64, 1)
        gain_sums.append(jnp.sum(grad * unit, axis=0, keepdims=True))
        grad = grad * gain
        grad = scale * (grad - unit * jnp.mean(grad * unit, axis=-1, keepdims=True))
        grad_qk[:, lanes] = grad.astype(jnp.bfloat16)
    grad_v[...] = grad_rotated[:, 768:].astype(jnp.bfloat16)
    gain_grads[0:1, :] = gain_sums[0] + gain_sums[1] + gain_sums[2] + gain_sums[3]
    gain_grads[1:2, :] = gain_sums[4] + gain_sums[5]
    gain_grads[2:8, :] = jnp.zeros((6, 128), jnp.float32)


def attend_backward(pre_qk, rotated, mixed, inverse, grad_mixed, q_gain, k_gain, cosine, sine, segment_rows, segment_columns):
    return pl.pallas_call(
        attend_backward_kernel,
        out_shape=(
            jax.ShapeDtypeStruct((512, 768), jnp.bfloat16),
            jax.ShapeDtypeStruct((512, 256), jnp.bfloat16),
            jax.ShapeDtypeStruct((8, 128), jnp.float32),
        ),
        scratch_shapes=[
            pltpu.VMEM((512, 512), jnp.bfloat16),
            pltpu.VMEM((512, 1024), jnp.float32),
            pltpu.VMEM((512, 512), jnp.float32),
        ],
        compiler_params=pltpu.CompilerParams(vmem_limit_bytes=28 * 1024 * 1024),
        cost_estimate=pl.CostEstimate(flops=1_700_000_000, bytes_accessed=8_000_000, transcendentals=700_000),
        name="attend_backward",
    )(pre_qk, rotated, mixed, inverse, grad_mixed, q_gain, k_gain, cosine, sine, segment_rows, segment_columns)


def core_pairs():
    return [(index, index ^ 1) for index in range(4)]


def chip_pairs():
    return [(index, index ^ 2) for index in range(4)]


def dp_shift(stage, step):
    pairs = []
    for z in range(4):
        for x in range(2):
            for y in range(4):
                target = {
                    "y": (z, x, (y + step) % 4),
                    "x": (z, (x + step) % 2, y),
                    "z": ((z + step) % 4, x, y),
                }[stage]
                pairs.append((z * 8 + x * 4 + y, target[0] * 8 + target[1] * 4 + target[2]))
    return pairs


def dp_place():
    index = lax.axis_index("dp")
    return {"z": index // 8, "x": index // 4 % 2, "y": index % 4}


def dp_groups(stage):
    groups = {}
    for z in range(4):
        for x in range(2):
            for y in range(4):
                key = {"z": (x, y), "y": (z, x)}[stage]
                groups.setdefault(key, []).append(z * 8 + x * 4 + y)
    return [groups[key] for key in sorted(groups)]


def column_ranges(widths):
    starts = [sum(widths[:index]) for index in range(len(widths))]
    return [pl.ds(start, width) for start, width in zip(starts, widths)]


def ring_gather(block, stage):
    return [(block, 0, None)] + [
        (lax.ppermute(block, "dp", dp_shift(stage, step)), step, None) for step in (1, 2, 3)
    ]


def two_step_gather(block, stage):
    half = block.shape[0] // 2
    below = lax.ppermute(block, "dp", dp_shift(stage, 1))
    above = lax.ppermute(block, "dp", dp_shift(stage, 3))
    far_low = lax.ppermute(below[:half], "dp", dp_shift(stage, 1))
    far_high = lax.ppermute(above[half:], "dp", dp_shift(stage, 3))
    return [(block, 0, None), (below, 1, None), (above, 3, None), (far_low, 2, 0), (far_high, 2, 1)]


def place_blocks(blocks, stage, shape, axis, widths):
    places = [(step, half) for _, step, half in blocks]

    def kernel(*refs):
        sources, targets, semaphores = refs[: len(places)], refs[len(places) : -1], refs[-1]
        index = lax.axis_index("dp")
        mine = index // 8 if stage == "z" else index % 4
        copies = []
        for order, (source, (step, half)) in enumerate(zip(sources, places)):
            spot = lax.rem(mine - step + 4, 4)
            rows = source.shape[0]
            rows = pl.ds(0 if half is None else half * rows, rows)
            for number, columns in enumerate(column_ranges(widths)):
                whole = targets[number]
                target = whole.at[spot, rows] if axis == 0 else whole.at[rows, spot]
                copies.append(
                    pltpu.make_async_copy(
                        source.at[..., columns], target, semaphores.at[order, number]
                    )
                )
        for copy in copies:
            copy.start()
        for copy in copies:
            copy.wait()

    arrays = [block for block, _, _ in blocks]
    return pl.pallas_call(
        kernel,
        out_shape=[jax.ShapeDtypeStruct((*shape, width), arrays[0].dtype) for width in widths],
        in_specs=[pl.BlockSpec(memory_space=pl.ANY)] * len(arrays),
        out_specs=[pl.BlockSpec(memory_space=pltpu.VMEM)] * len(widths),
        scratch_shapes=[pltpu.SemaphoreType.DMA((len(arrays), len(widths)))],
        compiler_params=pltpu.CompilerParams(vmem_limit_bytes=16 * 1024 * 1024),
        cost_estimate=pl.CostEstimate(
            flops=0, bytes_accessed=4 * math.prod(shape) * sum(widths), transcendentals=0
        ),
        name="place_blocks",
    )(*arrays)


def split_blocks(parts, stage, axis):
    widths = [part.shape[-1] for part in parts]
    lead = parts[0].shape[:-1]
    shape = (*lead[:axis], *lead[axis + 1 :], sum(widths))

    def kernel(*refs):
        sources, blocks, semaphores = refs[: len(parts)], refs[len(parts) : -1], refs[-1]
        index = lax.axis_index("dp")
        mine = index // 8 if stage == "z" else index % 4
        copies = []
        for step, block in enumerate(blocks):
            spot = lax.rem(mine + step, 4)
            for number, columns in enumerate(column_ranges(widths)):
                source = sources[number]
                piece = source.at[spot] if axis == 0 else source.at[:, spot]
                copies.append(
                    pltpu.make_async_copy(
                        piece, block.at[..., columns], semaphores.at[step, number]
                    )
                )
        for copy in copies:
            copy.start()
        for copy in copies:
            copy.wait()

    return pl.pallas_call(
        kernel,
        out_shape=[jax.ShapeDtypeStruct(shape, parts[0].dtype)] * 4,
        in_specs=[pl.BlockSpec(memory_space=pltpu.VMEM)] * len(parts),
        out_specs=[pl.BlockSpec(memory_space=pl.ANY)] * 4,
        scratch_shapes=[pltpu.SemaphoreType.DMA((4, len(parts)))],
        compiler_params=pltpu.CompilerParams(vmem_limit_bytes=16 * 1024 * 1024),
        cost_estimate=pl.CostEstimate(
            flops=0, bytes_accessed=16 * math.prod(shape), transcendentals=0
        ),
        name="split_blocks",
    )(*parts)


def join_x(block, other):
    return jnp.where(
        dp_place()["x"] == 0, jnp.stack([block, other]), jnp.stack([other, block])
    )


def gather_x(block, *side_work):
    return join_x(block, after(lax.ppermute(block, "dp", dp_shift("x", 1)), *side_work))


def place_first(blocks, stage, widths):
    if stage == "y":
        wholes = place_blocks(blocks, "y", (2, 4, 32), 1, widths)
    else:
        wholes = place_blocks(blocks, "z", (4, 2, 32), 0, widths)
    return [whole.reshape(256, width) for whole, width in zip(wholes, widths)]


def place_last(blocks, stage, widths):
    if stage == "z":
        wholes = place_blocks(blocks, "z", (4, 256), 0, widths)
    else:
        blocks = [
            (block.reshape(-1, 32, sum(widths)), step, half) for block, step, half in blocks
        ]
        wholes = place_blocks(blocks, "y", (8, 4, 32), 1, widths)
    return [whole.reshape(1024, width) for whole, width in zip(wholes, widths)]


def ring_send(blocks, stage):
    return [blocks[0]] + [
        lax.ppermute(blocks[step], "dp", dp_shift(stage, step)) for step in (1, 2, 3)
    ]


def ring_sum(sent):
    total = sum(block.astype(jnp.float32) for block in sent).astype(jnp.bfloat16)
    return total.reshape(256, total.shape[-1])


def split_first(parts, stage):
    if stage == "z":
        blocks = split_blocks([part.reshape(4, 256, -1) for part in parts], "z", 0)
    else:
        blocks = split_blocks([part.reshape(8, 4, 32, -1) for part in parts], "y", 1)
    return blocks


def x_parts(part, first_stage):
    width = part.shape[-1]
    if first_stage == "z":
        low, high = part[:128], part[128:]
    else:
        blocks = part.reshape(4, 2, 32, width)
        low, high = blocks[:, 0].reshape(128, width), blocks[:, 1].reshape(128, width)
    place = dp_place()["x"]
    return jnp.where(place == 0, low, high), jnp.where(place == 0, high, low)


def send_x(part, first_stage):
    return lax.ppermute(x_parts(part, first_stage)[1], "dp", dp_shift("x", 1))


def add_x(part, other, first_stage):
    kept = x_parts(part, first_stage)[0].astype(jnp.float32)
    return (kept + other.astype(jnp.float32)).astype(jnp.bfloat16)


def scatter_last(parts, stage):
    blocks = jnp.concatenate(parts, axis=1).reshape(4, 32, -1)
    mine = dp_place()[stage]
    total = lax.dynamic_index_in_dim(blocks, mine, 0, False).astype(jnp.float32)
    for step in (1, 2, 3):
        away = lax.dynamic_index_in_dim(blocks, (mine + step) % 4, 0, False)
        total = total + lax.ppermute(away, "dp", dp_shift(stage, step)).astype(jnp.float32)
    return total


def after(values, *others):
    return lax.optimization_barrier((values, others))[0]


def rms_scale(values, gain):
    return (
        values
        * lax.rsqrt(jnp.mean(values * values, axis=-1, keepdims=True) + NORM_EPS)
        * gain
    )


def rms_backward(values, gain, grad):
    scale = lax.rsqrt(jnp.mean(values * values, axis=-1, keepdims=True) + NORM_EPS)
    unit = values * scale
    scaled = grad * gain
    grad_values = scale * (scaled - unit * jnp.mean(scaled * unit, axis=-1, keepdims=True))
    return grad_values, jnp.sum(grad * unit, axis=0)


def dot(left, right):
    return jnp.dot(left, right, preferred_element_type=jnp.float32)


def dot_nt(left, right):
    return lax.dot_general(left, right, NT, preferred_element_type=jnp.float32)


def dot_tn(left, right):
    return lax.dot_general(left, right, TN, preferred_element_type=jnp.float32).astype(
        jnp.bfloat16
    )


def own_block(rows):
    chip = lax.axis_index("tensor") // 2
    blocks = rows.reshape(2, 128, rows.shape[-1])
    return jnp.where(chip == 0, blocks[0], blocks[1])


def both_blocks(block, *side_work):
    chip = lax.axis_index("tensor") // 2
    other = after(lax.ppermute(block, "tensor", chip_pairs()), *side_work)
    return jnp.where(
        chip == 0, jnp.concatenate([block, other]), jnp.concatenate([other, block])
    )


def with_sibling(rows):
    return jnp.concatenate([rows, lax.ppermute(rows, "tensor", core_pairs())])


def sum_cores(term):
    away = lax.ppermute(term(1).astype(jnp.bfloat16), "tensor", core_pairs())
    return (term(0) + away.astype(jnp.float32)).astype(jnp.bfloat16)


def sum_chips(part, *side_work):
    other = after(lax.ppermute(part, "tensor", chip_pairs()), *side_work)
    return part.astype(jnp.float32) + other.astype(jnp.float32)


def sum_own_block(part):
    chip = lax.axis_index("tensor") // 2
    part = part.reshape(2, 128, -1)
    keep = jnp.where(chip == 0, part[0], part[1])
    send = jnp.where(chip == 0, part[1], part[0])
    other = lax.ppermute(send, "tensor", chip_pairs())
    return keep.astype(jnp.float32) + other.astype(jnp.float32)


def halves(array):
    return (array[:256], array[256:])


def rotary_tables(segment_ids):
    width = segment_ids.shape[0]
    core = lax.axis_index("tensor") % 2
    column = jnp.arange(width, dtype=jnp.int32)
    doc_starts = jnp.zeros((width,), jnp.int32)
    for doc_number in range(4):
        before = jnp.sum((segment_ids < doc_number).astype(jnp.int32))
        doc_starts = doc_starts + jnp.where(segment_ids == doc_number, before, 0)
    blocks = (column - doc_starts).astype(jnp.float32).reshape(2, 2, 128)
    position = jnp.where(
        core == 0,
        jnp.concatenate([blocks[:, 0], blocks[:, 1]]),
        jnp.concatenate([blocks[:, 1], blocks[:, 0]]),
    ).reshape(width)
    frequency = jnp.exp(
        jnp.arange(HEAD // 2, dtype=jnp.float32) * (-2.0 * math.log(ROPE_BASE) / HEAD)
    )
    angles = position[:, None] * frequency[None, :]
    cosine, sine = jnp.cos(angles), jnp.sin(angles)
    return (
        jnp.concatenate([cosine, cosine], axis=-1),
        jnp.concatenate([-sine, sine], axis=-1),
    )


def send_direct(blocks):
    return lax.all_to_all(blocks, "dp", 0, 0, tiled=True)


def sum_sent(sent):
    return jnp.sum(sent.reshape(32, 32, -1).astype(jnp.float32), axis=0)


def body(
    tokens,
    segment_ids,
    cotangent,
    attn_norm,
    q_weight,
    key_projection,
    value_projection,
    o_weight,
    q_gain,
    k_gain,
    mlp_norm,
    gate_weight,
    up_weight,
    down_weight,
):
    attend = gather_x(
        jnp.concatenate(
            [q_weight[0], key_projection[0], value_projection[0], o_weight[0].T], axis=1
        )
    )
    rest = after((gate_weight, up_weight, down_weight, o_weight, tokens, segment_ids), attend)
    gate_weight, up_weight, down_weight, o_weight, tokens, segment_ids = rest
    qk_part = place_first(ring_gather(attend[..., :768], "y"), "y", [768])[0]
    vo_part = place_first(ring_gather(attend[..., 768:], "z"), "z", [768])[0]
    (wqk,) = place_last(ring_gather(qk_part, "z"), "z", [768])
    wv, wo = place_last(ring_gather(vo_part, "y"), "y", [256, 512])

    feed = jnp.concatenate([gate_weight[0], up_weight[0], down_weight[0].T], axis=1)
    feed = gather_x(feed)
    gate_up_part = place_first(ring_gather(feed[..., :1536], "z"), "z", [1536])[0]
    down_part = place_first(ring_gather(feed[..., 1536:], "y"), "y", [768])[0]
    wg, wu = place_last(two_step_gather(gate_up_part, "y"), "y", [768, 768])
    (wd,) = place_last(two_step_gather(down_part, "z"), "z", [768])

    second = [
        q_weight[1],
        key_projection[1],
        value_projection[1],
        o_weight[1].T,
        down_weight[1].T,
        gate_weight[1],
        up_weight[1],
    ]
    second = gather_x(jnp.concatenate(second, axis=1))
    next_attend, next_down = place_first(
        ring_gather(second[..., :2304], "y"), "y", [1536, 768]
    )
    next_gate_up = place_first(ring_gather(second[..., 2304:], "z"), "z", [1536])[0]
    next_wqk, next_wv, next_wo = place_last(
        two_step_gather(next_attend, "z"), "z", [768, 256, 512]
    )
    next_wg, next_wu = place_last(two_step_gather(next_gate_up, "y"), "y", [768, 768])
    (next_wd,) = place_last(two_step_gather(next_down, "z"), "z", [768])
    attend_weights = [(wqk, wv, wo), (next_wqk, next_wv, next_wo)]
    feed_weights = [(wg, wu, wd), (next_wg, next_wu, next_wd)]

    cosine, sine = rotary_tables(segment_ids)
    segment_rows, segment_columns = segment_ids[:, None], segment_ids[None, :]
    residual = both_blocks(tokens).astype(jnp.float32)
    first_normed = rms_scale(residual, attn_norm[0]).astype(jnp.bfloat16)
    grad_rows = both_blocks(after(cotangent, first_normed)).astype(jnp.float32)
    saved_layers = []
    for layer in range(2):
        wqk, wv, wo = attend_weights[layer]
        gains = (q_gain[layer][None], k_gain[layer][None])
        if layer == 1:
            first_normed = rms_scale(residual, attn_norm[1]).astype(jnp.bfloat16)
        normed = with_sibling(first_normed)
        pre_qk, pre_v = dot(normed, wqk), dot(normed, wv)
        rotated, mixed, inverse = attend_forward(
            pre_qk, pre_v, *gains, cosine, sine, segment_rows, segment_columns
        )
        mixed_halves = halves(mixed)
        part = sum_cores(lambda side: dot_nt(mixed_halves[side], wo))
        middle = residual + sum_chips(part)
        normed_two = with_sibling(rms_scale(middle, mlp_norm[layer]).astype(jnp.bfloat16))
        wg, wu, wd = feed_weights[layer]
        gate, up = dot(normed_two, wg), dot(normed_two, wu)
        product = (jax.nn.silu(gate) * up).astype(jnp.bfloat16)
        product_halves = halves(product)
        saved_layers.append(
            (residual, middle, normed, normed_two, pre_qk, rotated, mixed, inverse, gate, up, product)
        )
        part = sum_cores(lambda side: dot_nt(product_halves[side], wd))
        if layer == 0:
            residual = middle + sum_chips(part)
        else:
            output = own_block(middle) + sum_own_block(part)
    output = output.astype(jnp.bfloat16)
    gain_grads = [None, None]
    for layer in (1, 0):
        wqk, wv, wo = attend_weights[layer]
        wg, wu, wd = feed_weights[layer]
        gains = (q_gain[layer][None], k_gain[layer][None])
        residual, middle, normed, normed_two, pre_qk, rotated, mixed, inverse, gate, up, product = (
            saved_layers[layer]
        )
        grad_out = with_sibling(grad_rows.astype(jnp.bfloat16))
        grad_product = dot(grad_out, wd)
        sigmoid = jax.nn.sigmoid(gate)
        grad_gate = grad_product * up * sigmoid * (1.0 + gate * (1.0 - sigmoid))
        grad_gate = grad_gate.astype(jnp.bfloat16)
        grad_up = (grad_product * gate * sigmoid).astype(jnp.bfloat16)
        gate_halves, up_halves = halves(grad_gate), halves(grad_up)
        part = sum_cores(
            lambda side: dot_nt(gate_halves[side], wg) + dot_nt(up_halves[side], wu)
        )
        down_grad = dot_tn(after(grad_out, part), product)
        normed_later = after(normed_two, part)
        gate_grad, up_grad = dot_tn(normed_later, grad_gate), dot_tn(normed_later, grad_up)
        if layer == 1:
            feed_blocks = split_first([gate_grad, up_grad, down_grad], "y")
            feed_sent = ring_send(feed_blocks, "y")
            side_work = feed_blocks
        else:
            gate_up_blocks = split_first([gate_grad, up_grad], "y")
            gate_up_sent = ring_send(gate_up_blocks, "y")
            feed_sum = ring_sum(after(feed_sent, part))
            feed_other = send_x(feed_sum, "y")
            side_work = [*gate_up_blocks, down_grad, feed_sum]
        grad_normed_two = sum_chips(part, *side_work)
        grad_middle, mlp_gain_grad = rms_backward(middle, mlp_norm[layer], grad_normed_two)
        grad_middle = grad_rows + grad_middle
        grad_branch = with_sibling(grad_middle.astype(jnp.bfloat16))
        grad_mixed = dot(grad_branch, wo).astype(jnp.bfloat16)
        o_grad = dot_tn(grad_branch, mixed)
        if layer == 0:
            o_down_sent = ring_send(split_first([o_grad, down_grad], "z"), "z")
        grad_qk, grad_v, gain_grad = attend_backward(
            pre_qk,
            rotated,
            mixed,
            inverse,
            grad_mixed,
            *gains,
            cosine,
            sine,
            segment_rows,
            segment_columns,
        )
        qk_halves, v_halves = halves(grad_qk), halves(grad_v)
        terms = [dot_nt(qk_halves[side], wqk) + dot_nt(v_halves[side], wv) for side in range(2)]
        part = sum_cores(lambda side: terms[side])
        normed_later = after(normed, part)
        qk_grad, v_grad = dot_tn(normed_later, grad_qk), dot_tn(normed_later, grad_v)
        if layer == 1:
            attend_blocks = split_first([qk_grad, v_grad, o_grad], "z")
            attend_sent = ring_send(attend_blocks, "z")
            grad_in, attn_gain_grad = rms_backward(
                residual, attn_norm[1], sum_chips(part, *attend_blocks)
            )
            attn_gain_grad = 0.5 * attn_gain_grad
            grad_rows = grad_middle + grad_in
        else:
            normed_halves = halves(normed)
            attn_gain_grad = sum(
                jnp.sum(terms[side] * normed_halves[side].astype(jnp.float32), axis=0)
                for side in range(2)
            )
            attn_gain_grad = attn_gain_grad / attn_norm[0]
        gain_grads[layer] = (attn_gain_grad, gain_grad[0], gain_grad[1], 0.5 * mlp_gain_grad)
    gain_block = jnp.concatenate([*gain_grads[0], *gain_grads[1]]).reshape(36, 128)
    gain_block = jnp.pad(gain_block, ((0, 28), (0, 0))).reshape(32, 256).astype(jnp.bfloat16)
    last = jnp.concatenate([qk_grad, v_grad, jnp.tile(gain_block, (32, 1))], axis=1)
    last_sent = send_direct(last)
    grad_in, _ = rms_backward(own_block(residual), attn_norm[0], sum_own_block(part))
    input_grad = own_block(grad_middle) + grad_in
    attend_sum = ring_sum(after(attend_sent, grad_qk))
    attend_other = send_x(attend_sum, "z")
    gate_up_sum = ring_sum(after(gate_up_sent, last))
    gate_up_other = send_x(gate_up_sum, "y")
    o_down_sum = ring_sum(after(o_down_sent, last))
    o_down_other = send_x(o_down_sum, "z")
    feed_other, attend_other = after((feed_other, attend_other), gate_up_sum, o_down_sum)
    y_own = scatter_last(
        [add_x(gate_up_sum, gate_up_other, "y"), add_x(feed_sum, feed_other, "y")], "z"
    )
    z_own = scatter_last(
        [add_x(o_down_sum, o_down_other, "z"), add_x(attend_sum, attend_other, "z")], "y"
    )
    last = sum_sent(last_sent)
    gain_sums = last[:, 1024:].reshape(64, 128)[:36]
    gain_sums = gain_sums + lax.ppermute(gain_sums, "tensor", core_pairs())
    gain_sums = gain_sums + lax.ppermute(gain_sums, "tensor", chip_pairs())
    gain_sums = gain_sums.reshape(2, 2304)
    first_gate, first_up, gate, up, down = jnp.split(y_own, [768, 1536, 2304, 3072], axis=1)
    first_o, first_down, qk, v, o = jnp.split(z_own, [512, 1280, 2048, 2304], axis=1)
    return (
        output,
        input_grad,
        gain_sums[:, :1024],
        jnp.stack([last[:, :512], qk[:, :512]]),
        jnp.stack([last[:, 512:768], qk[:, 512:]]),
        jnp.stack([last[:, 768:1024], v]),
        jnp.stack([first_o.T, o.T]),
        gain_sums[:, 1024:1152],
        gain_sums[:, 1152:1280],
        gain_sums[:, 1280:],
        jnp.stack([first_gate, gate]),
        jnp.stack([first_up, up]),
        jnp.stack([first_down.T, down.T]),
    )


def solution(mesh):
    rows = P(("dp", "tensor"), None)
    in_rows, in_columns = P(None, "dp", "tensor"), P(None, "tensor", "dp")
    return jax.shard_map(
        body,
        mesh=mesh,
        in_specs=(
            rows,
            P("dp"),
            rows,
            P(),
            in_rows,
            in_rows,
            in_rows,
            in_columns,
            P(),
            P(),
            P(),
            in_rows,
            in_rows,
            in_columns,
        ),
        out_specs=(
            rows,
            rows,
            P(),
            in_rows,
            in_rows,
            in_rows,
            in_columns,
            P(),
            P(),
            P(),
            in_rows,
            in_rows,
            in_columns,
        ),
        check_vma=False,
    )
```

time: 4370 us -> 500 us (0.11)
  the two profiles are of different devices: /device:TPU:0 before, /device:TPU:2 now
where the time goes in v2:
time: 500 us; the launch traced here: 490 us
  waiting for transfers between devices  214 us (43%)
  starting transfers between devices  137 us (27%)
  matrix products  43 us (9%)
  other arithmetic  39 us (8%)
  Pallas kernels  27.8 us (6%)
  local copies, waits for them, and re-layouts  25.7 us (5%)
    ppermute x12, waiting for transfers between devices, ring_send(): lax.ppermute(blocks[step], 'dp', dp_shift(stage, step))  53.3 us
    ppermute x24, starting transfers between devices, ring_gather(): lax.ppermute(block, 'dp', dp_shift(stage, step))  39.7 us
    ppermute x24, waiting for transfers between devices, ring_gather(): lax.ppermute(block, 'dp', dp_shift(stage, step))  39.7 us
    ppermute x5, waiting for transfers between devices, two_step_gather(): below = lax.ppermute(block, 'dp', dp_shift(stage, 1))  34 us
    ppermute x6, waiting for transfers between devices, sum_chips(): other = after(lax.ppermute(part, 'tensor', chip_pairs()), *side_work)  25.3 us
    ppermute x5, waiting for transfers between devices, two_step_gather(): far_low = lax.ppermute(below[:half], 'dp', dp_shift(stage, 1))  18.9 us
    unnamed x202, local copies, waits for them, and re-layouts  18.2 us
    ppermute x12, starting transfers between devices, ring_send(): lax.ppermute(blocks[step], 'dp', dp_shift(stage, step))  18.1 us
  transfers between devices with their start and end apart: 98, of which 39 were waited for; matrix products, arithmetic and copies ran while one was open for 14% of the time, Pallas kernels for 4%

profile of v2, /device:TPU:2, one launch (start us, length us, event | category | flops | bytes accessed | tf_op | source)
XLA Modules:
  0.0 489.9 jit_solution(2048548345203431526)
XLA Ops:
  5.1 2.6 collective-permute-done
  9.7 3.6 collective-permute-start.10
  19.4 3.3 subtract_convert_fusion
  24.5 3.0 collective-permute-start.4
  35.7 12.1 %collective-permute-done.12 = bf16[256,768]{1,0:T(8,128)(2,1)S(1)} collective-permute-done((bf16[256,768]{1,0:T(8,128)(2,1)S(1)}, bf16[256,768]{1,0:T(8,128)(2,1)S(1)}, u32[]{:S(2)}, u32[]{:S(2)}) %collective-permute-start.12) | collective-permute-done | bytes 393248 | tf_op jit(solution)/shard_map/ppermute | solution.py:225
  49.2 3.0 collective-permute-start.8
  68.6 3.2 attend_forward.2
  74.4 4.8 collective-permute-done.18
  88.8 3.3 collective-permute-start.20
  94.5 2.9 collective-permute-start.30
  97.9 4.4 collective-permute-done.21.refs_3_
  103.4 3.2 collective-permute-start.23
  107.3 13.9 %collective-permute-done.22 = bf16[256,1536]{1,0:T(8,128)(2,1)S(1)} collective-permute-done((bf16[256,1536]{1,0:T(8,128)(2,1)S(1)}, bf16[256,1536]{1,0:T(8,128)(2,1)S(1)}, u32[]{:S(2)}, u32[]{:S(2)}) %collective-permute-start.22) | collective-permute-done | bytes 786464 | tf_op jit(solution)/shard_map/ppermute | solution.py:231
  121.4 3.3 collective-permute-start.25
  128.6 3.5 collective-permute-done.31.refs_3_
  140.4 6.9 %collective-permute-done.36 = bf16[32,3840]{1,0:T(8,128)(2,1)S(1)} collective-permute-done((bf16[32,3840]{1,0:T(8,128)(2,1)S(1)}, bf16[32,3840]{1,0:T(8,128)(2,1)S(1)}, u32[]{:S(2)}, u32[]{:S(2)}) %collective-permute-start.36) | collective-permute-done | bytes 245792 | tf_op jit(solution)/shard_map/ppermute | solution.py:324
  153.6 12.3 %collective-permute-done.37.refs_1_ = bf16[2,32,2304]{2,1,0:T(8,128)(2,1)S(1)} collective-permute-done((bf16[2,32,2304]{2,1,0:T(8,128)(2,1)S(1)}, bf16[2,32,2304]{2,1,0:T(8,128)(2,1)S(1)}, u32[]{:S(2)}, u32[]{:S(2)}) %collective-permute-start.37) | collective-permute-done | bytes 294944 | tf_op jit(solution)/shard_map/ppermute | solution.py:225
  168.4 2.6 collective-permute-start.41
  171.5 15.2 %collective-permute-done.40.refs_1_ = bf16[256,1536]{1,0:T(8,128)(2,1)S(1)} collective-permute-done((bf16[256,1536]{1,0:T(8,128)(2,1)S(1)}, bf16[256,1536]{1,0:T(8,128)(2,1)S(1)}, u32[]{:S(2)}, u32[]{:S(2)}) %collective-permute-start.40) | collective-permute-done | bytes 786464 | tf_op jit(solution)/shard_map/ppermute | solution.py:231
  186.8 3.3 collective-permute-start.43
  190.1 6.3 %collective-permute-done.42.refs_3_ = bf16[128,1536]{1,0:T(8,128)(2,1)S(1)} collective-permute-done((bf16[128,1536]{1,0:T(8,128)(2,1)S(1)}, bf16[128,1536]{1,0:T(8,128)(2,1)S(1)}, u32[]{:S(2)}, u32[]{:S(2)}) %collective-permute-start.42) | collective-permute-done | bytes 393248 | tf_op jit(solution)/shard_map/ppermute | solution.py:233
  199.4 3.3 attend_forward.3
  206.5 4.2 collective-permute-start.48
  214.8 5.4 %collective-permute-done.48.refs_2_ = bf16[2,32,1536]{2,1,0:T(8,128)(2,1)} collective-permute-done((bf16[2,32,1536]{2,1,0:T(8,128)(2,1)}, bf16[2,32,1536]{2,1,0:T(8,128)(2,1)}, u32[]{:S(2)}, u32[]{:S(2)}) %collective-permute-start.48) | collective-permute-done | bytes 196640 | tf_op jit(solution)/shard_map/ppermute | solution.py:225
  221.4 3.8 collective-permute-start.50
  228.9 2.6 collective-permute-start.55
  233.0 5.0 %collective-permute-done.54.refs_1_ = bf16[256,768]{1,0:T(8,128)(2,1)S(1)} collective-permute-done((bf16[256,768]{1,0:T(8,128)(2,1)S(1)}, bf16[256,768]{1,0:T(8,128)(2,1)S(1)}, u32[]{:S(2)}, u32[]{:S(2)}) %collective-permute-start.54) | collective-permute-done | bytes 393248 | tf_op jit(solution)/shard_map/ppermute | solution.py:231
  241.5 3.2 collective-permute-start.57
  246.0 2.9 collective-permute-done.56.refs_3_
  250.8 2.7 collective-permute-start.53
  255.0 6.2 %collective-permute-done.52 = bf16[128,1536]{1,0:T(8,128)(2,1)S(1)} collective-permute-done((bf16[128,1536]{1,0:T(8,128)(2,1)S(1)}, bf16[128,1536]{1,0:T(8,128)(2,1)S(1)}, u32[]{:S(2)}, u32[]{:S(2)}) %collective-permute-start.52) | collective-permute-done | bytes 393248 | tf_op jit(solution)/shard_map/ppermute | solution.py:233
  276.4 4.3 collective-permute-start.83
  281.2 4.4 collective-permute-done.63
  290.4 4.8 attend_backward.2
  303.3 12.4 %collective-permute-done.66 = bf16[256,1024]{1,0:T(8,128)(2,1)S(1)} collective-permute-done((bf16[256,1024]{1,0:T(8,128)(2,1)S(1)}, bf16[256,1024]{1,0:T(8,128)(2,1)S(1)}, u32[]{:S(2)}, u32[]{:S(2)}) %collective-permute-start.66) | collective-permute-done | bytes 524320 | tf_op jit(solution)/shard_map/ppermute | solution.py:453
  323.8 3.3 collective-permute-start.80
  337.5 8.4 %collective-permute-done.69 = bf16[256,1024]{1,0:T(8,128)(2,1)S(1)} collective-permute-done((bf16[256,1024]{1,0:T(8,128)(2,1)S(1)}, bf16[256,1024]{1,0:T(8,128)(2,1)S(1)}, u32[]{:S(2)}, u32[]{:S(2)}) %collective-permute-start.69) | collective-permute-done | bytes 524320 | tf_op jit(solution)/shard_map/ppermute | solution.py:453
  352.2 4.7 attend_backward.3
  374.1 8.5 %all-to-all-start = ((bf16[32,32,1280]{2,1,0:T(8,128)(2,1)}), bf16[32,32,1280]{2,1,0:T(8,128)(2,1)}, u32[]{:S(2)}, u32[]{:S(2)}) async-start(bf16[32,32,1280]{2,1,0:T(8,128)(2,1)} %pad_maximum_fusion), calls=%async_computation | async-start | bytes 5242880 | tf_op jit(solution)/shard_map/all_to_all | solution.py:496
  384.2 2.7 collective-permute-start.76
  386.9 13.9 %collective-permute-done.92 = bf16[8,32,1536]{2,1,0:T(8,128)(2,1)} collective-permute-done((bf16[8,32,1536]{2,1,0:T(8,128)(2,1)}, bf16[8,32,1536]{2,1,0:T(8,128)(2,1)}, u32[]{:S(2)}, u32[]{:S(2)}) %collective-permute-start.92) | collective-permute-done | bytes 786464 | tf_op jit(solution)/shard_map/ppermute | solution.py:348
  402.9 25.9 %collective-permute-done.75 = bf16[256,1280]{1,0:T(8,128)(2,1)S(1)} collective-permute-done((bf16[256,1280]{1,0:T(8,128)(2,1)S(1)}, bf16[256,1280]{1,0:T(8,128)(2,1)S(1)}, u32[]{:S(2)}, u32[]{:S(2)}) %collective-permute-start.75) | collective-permute-done | bytes 655392 | tf_op jit(solution)/shard_map/ppermute | solution.py:348
  429.9 12.5 %collective-permute-done.76 = bf16[256,1280]{1,0:T(8,128)(2,1)S(1)} collective-permute-done((bf16[256,1280]{1,0:T(8,128)(2,1)S(1)}, bf16[256,1280]{1,0:T(8,128)(2,1)S(1)}, u32[]{:S(2)}, u32[]{:S(2)}) %collective-permute-start.76) | collective-permute-done | bytes 655392 | tf_op jit(solution)/shard_map/ppermute | solution.py:348
  448.8 5.7 %collective-permute-done.93 = bf16[128,1536]{1,0:T(8,128)(2,1)S(1)} collective-permute-done((bf16[128,1536]{1,0:T(8,128)(2,1)S(1)}, bf16[128,1536]{1,0:T(8,128)(2,1)S(1)}, u32[]{:S(2)}, u32[]{:S(2)}) %collective-permute-start.93) | collective-permute-done | bytes 393248 | tf_op jit(solution)/shard_map/ppermute | solution.py:377
  454.7 4.7 collective-permute-done.78
  459.6 2.6 collective-permute-start.89
  465.3 3.4 collective-permute-done.89
  484.8 3.5 collective-permute-done.74
  (547 shorter events, 205.0 us)
Async XLA Ops:
  7.7 16.8 %collective-permute-start.9 = (bf16[2,32,768]{2,1,0:T(8,128)(2,1)S(1)}, bf16[2,32,768]{2,1,0:T(8,128)(2,1)S(1)}, u32[]{:S(2)}, u32[]{:S(2)}) collective-permute-start(bf16[2,32,768]{2,1,0:T(8,128)(2,1)S(1)} %get-tuple-element.211.refs_0_), channel_id=1, source_target_pairs={{0,32},{4,36},{8,40},{12,44},{16,48},{20,52},{24,56},{28,60},{32,6... | collective-permute-start | bytes 294920 | tf_op jit(solution)/shard_map/ppermute | solution.py:225
  9.7 17.8 %collective-permute-start.10 = (bf16[2,32,768]{2,1,0:T(8,128)(2,1)S(1)}, bf16[2,32,768]{2,1,0:T(8,128)(2,1)S(1)}, u32[]{:S(2)}, u32[]{:S(2)}) collective-permute-start(bf16[2,32,768]{2,1,0:T(8,128)(2,1)S(1)} %get-tuple-element.211.refs_0_), channel_id=1, source_target_pairs={{0,64},{4,68},{8,72},{12,76},{16,80},{20,84},{24,88},{28,92},{32,9... | collective-permute-start | bytes 294920 | tf_op jit(solution)/shard_map/ppermute | solution.py:225
  13.3 15.6 %collective-permute-start.11 = (bf16[2,32,768]{2,1,0:T(8,128)(2,1)S(1)}, bf16[2,32,768]{2,1,0:T(8,128)(2,1)S(1)}, u32[]{:S(2)}, u32[]{:S(2)}) collective-permute-start(bf16[2,32,768]{2,1,0:T(8,128)(2,1)S(1)} %get-tuple-element.211.refs_0_), channel_id=1, source_target_pairs={{0,96},{4,100},{8,104},{12,108},{16,112},{20,116},{24,120},{28,124... | collective-permute-start | bytes 294920 | tf_op jit(solution)/shard_map/ppermute | solution.py:225
  14.3 17.9 %collective-permute-start.3 = (bf16[2,32,768]{2,1,0:T(8,128)(2,1)S(1)}, bf16[2,32,768]{2,1,0:T(8,128)(2,1)S(1)}, u32[]{:S(2)}, u32[]{:S(2)}) collective-permute-start(bf16[2,32,768]{2,1,0:T(8,128)(2,1)S(1)} %get-tuple-element.210.refs_0_), channel_id=1, source_target_pairs={{0,4},{4,8},{8,12},{12,0},{16,20},{20,24},{24,28},{28,16},{32,36},... | collective-permute-start | bytes 294920 | tf_op jit(solution)/shard_map/ppermute | solution.py:225
  29.4 18.3 %collective-permute-start.12 = (bf16[256,768]{1,0:T(8,128)(2,1)S(1)}, bf16[256,768]{1,0:T(8,128)(2,1)S(1)}, u32[]{:S(2)}, u32[]{:S(2)}) collective-permute-start(bf16[256,768]{1,0:T(8,128)(2,1)S(1)} %bitcast.293), channel_id=1, source_target_pairs={{0,4},{4,8},{8,12},{12,0},{16,20},{20,24},{24,28},{28,16},{32,36},... | collective-permute-start | bytes 1179656 | tf_op jit(solution)/shard_map/ppermute | solution.py:225
  30.2 18.3 %collective-permute-start.13 = (bf16[256,768]{1,0:T(8,128)(2,1)S(1)}, bf16[256,768]{1,0:T(8,128)(2,1)S(1)}, u32[]{:S(2)}, u32[]{:S(2)}) collective-permute-start(bf16[256,768]{1,0:T(8,128)(2,1)S(1)} %bitcast.294), channel_id=1, source_target_pairs={{0,8},{4,12},{8,0},{12,4},{16,24},{20,28},{24,16},{28,20},{32,40},... | collective-permute-start | bytes 1179656 | tf_op jit(solution)/shard_map/ppermute | solution.py:225
  32.2 31.9 %collective-permute-start.2 = (bf16[256,1024]{1,0:T(8,128)(2,1)}, bf16[256,1024]{1,0:T(8,128)(2,1)}, u32[]{:S(2)}, u32[]{:S(2)}) collective-permute-start(bf16[256,1024]{1,0:T(8,128)(2,1)} %multiply_convert_fusion.9), channel_id=1, source_target_pairs={{0,1},{1,0},{2,3},{3,2},{4,5},{5,4},{6,7},{7,6},{8,9},{9,8},{10,11... | collective-permute-start | bytes 1572872 | tf_op jit(solution)/shard_map/ppermute | solution.py:444
  32.3 22.3 %collective-permute-start.14 = (bf16[256,768]{1,0:T(8,128)(2,1)S(1)}, bf16[256,768]{1,0:T(8,128)(2,1)}, u32[]{:S(2)}, u32[]{:S(2)}) collective-permute-start(bf16[256,768]{1,0:T(8,128)(2,1)S(1)} %bitcast.295), channel_id=1, source_target_pairs={{0,12},{4,0},{8,4},{12,8},{16,28},{20,16},{24,20},{28,24},{32,44},... | collective-permute-start | bytes 1179656 | tf_op jit(solution)/shard_map/ppermute | solution.py:225
  34.6 23.2 %collective-permute-start.6 = (bf16[256,768]{1,0:T(8,128)(2,1)S(1)}, bf16[256,768]{1,0:T(8,128)(2,1)S(1)}, u32[]{:S(2)}, u32[]{:S(2)}) collective-permute-start(bf16[256,768]{1,0:T(8,128)(2,1)S(1)} %bitcast.289), channel_id=1, source_target_pairs={{0,32},{4,36},{8,40},{12,44},{16,48},{20,52},{24,56},{28,60},{32,6... | collective-permute-start | bytes 1179656 | tf_op jit(solution)/shard_map/ppermute | solution.py:225
  79.7 27.0 %collective-permute-start.16 = (bf16[256,1024]{1,0:T(8,128)(2,1)S(1)}, bf16[256,1024]{1,0:T(8,128)(2,1)S(1)}, u32[]{:S(2)}, u32[]{:S(2)}) collective-permute-start(bf16[256,1024]{1,0:T(8,128)(2,1)S(1)} %fusion.8), channel_id=1, source_target_pairs={{0,2},{1,3},{2,0},{3,1},{4,6},{5,7},{6,4},{7,5},{8,10},{9,11},{10,... | collective-permute-start | bytes 1572872 | tf_op jit(solution)/shard_map/ppermute | solution.py:453
  94.1 30.6 %collective-permute-start.29 = (bf16[256,768]{1,0:T(8,128)(2,1)S(1)}, bf16[256,768]{1,0:T(8,128)(2,1)S(1)}, u32[]{:S(2)}, u32[]{:S(2)}) collective-permute-start(bf16[256,768]{1,0:T(8,128)(2,1)S(1)} %bitcast.286), channel_id=1, source_target_pairs={{0,32},{4,36},{8,40},{12,44},{16,48},{20,52},{24,56},{28,60},{32,6... | collective-permute-start | bytes 1179656 | tf_op jit(solution)/shard_map/ppermute | solution.py:231
  94.5 32.8 %collective-permute-start.30 = (bf16[256,768]{1,0:T(8,128)(2,1)S(1)}, bf16[256,768]{1,0:T(8,128)(2,1)S(1)}, u32[]{:S(2)}, u32[]{:S(2)}) collective-permute-start(bf16[256,768]{1,0:T(8,128)(2,1)S(1)} %bitcast.287), channel_id=1, source_target_pairs={{0,96},{4,100},{8,104},{12,108},{16,112},{20,116},{24,120},{28,124... | collective-permute-start | bytes 1179656 | tf_op jit(solution)/shard_map/ppermute | solution.py:232
  103.3 17.9 %collective-permute-start.22 = (bf16[256,1536]{1,0:T(8,128)(2,1)S(1)}, bf16[256,1536]{1,0:T(8,128)(2,1)S(1)}, u32[]{:S(2)}, u32[]{:S(2)}) collective-permute-start(bf16[256,1536]{1,0:T(8,128)(2,1)S(1)} %bitcast.263), channel_id=1, source_target_pairs={{0,4},{4,8},{8,12},{12,0},{16,20},{20,24},{24,28},{28,16},{32,36},... | collective-permute-start | bytes 2359304 | tf_op jit(solution)/shard_map/ppermute | solution.py:231
  103.4 18.0 %collective-permute-start.23 = (bf16[256,1536]{1,0:T(8,128)(2,1)S(1)}, bf16[256,1536]{1,0:T(8,128)(2,1)S(1)}, u32[]{:S(2)}, u32[]{:S(2)}) collective-permute-start(bf16[256,1536]{1,0:T(8,128)(2,1)S(1)} %bitcast.264), channel_id=1, source_target_pairs={{0,12},{4,0},{8,4},{12,8},{16,28},{20,16},{24,20},{28,24},{32,44},... | collective-permute-start | bytes 2359304 | tf_op jit(solution)/shard_map/ppermute | solution.py:232
  107.2 27.3 %collective-permute-start.17 = (bf16[256,1024]{1,0:T(8,128)(2,1)S(1)}, bf16[256,1024]{1,0:T(8,128)(2,1)S(1)}, u32[]{:S(2)}, u32[]{:S(2)}) collective-permute-start(bf16[256,1024]{1,0:T(8,128)(2,1)S(1)} %multiply_convert_fusion.8), channel_id=1, source_target_pairs={{0,1},{1,0},{2,3},{3,2},{4,5},{5,4},{6,7},{7,6},{8,9},{9,8},{10,11... | collective-permute-start | bytes 1572872 | tf_op jit(solution)/shard_map/ppermute | solution.py:444
  148.0 23.0 %collective-permute-start.34 = (bf16[256,1024]{1,0:T(8,128)(2,1)S(1)}, bf16[256,1024]{1,0:T(8,128)(2,1)S(1)}, u32[]{:S(2)}, u32[]{:S(2)}) collective-permute-start(bf16[256,1024]{1,0:T(8,128)(2,1)S(1)} %fusion.3), channel_id=1, source_target_pairs={{0,2},{1,3},{2,0},{3,1},{4,6},{5,7},{6,4},{7,5},{8,10},{9,11},{10,... | collective-permute-start | bytes 1572872 | tf_op jit(solution)/shard_map/ppermute | solution.py:453
  150.3 15.6 %collective-permute-start.37 = (bf16[2,32,2304]{2,1,0:T(8,128)(2,1)S(1)}, bf16[2,32,2304]{2,1,0:T(8,128)(2,1)S(1)}, u32[]{:S(2)}, u32[]{:S(2)}) collective-permute-start(bf16[2,32,2304]{2,1,0:T(8,128)(2,1)S(1)} %slice.441.refs_0_), channel_id=1, source_target_pairs={{0,4},{4,8},{8,12},{12,0},{16,20},{20,24},{24,28},{28,16},{32,36},... | collective-permute-start | bytes 884744 | tf_op jit(solution)/shard_map/ppermute | solution.py:225
  150.4 15.5 %collective-permute-start.38 = (bf16[2,32,2304]{2,1,0:T(8,128)(2,1)S(1)}, bf16[2,32,2304]{2,1,0:T(8,128)(2,1)S(1)}, u32[]{:S(2)}, u32[]{:S(2)}) collective-permute-start(bf16[2,32,2304]{2,1,0:T(8,128)(2,1)S(1)} %slice.441.refs_0_), channel_id=1, source_target_pairs={{0,8},{4,12},{8,0},{12,4},{16,24},{20,28},{24,16},{28,20},{32,40},... | collective-permute-start | bytes 884744 | tf_op jit(solution)/shard_map/ppermute | solution.py:225
  151.9 14.6 %collective-permute-start.39 = (bf16[2,32,2304]{2,1,0:T(8,128)(2,1)S(1)}, bf16[2,32,2304]{2,1,0:T(8,128)(2,1)S(1)}, u32[]{:S(2)}, u32[]{:S(2)}) collective-permute-start(bf16[2,32,2304]{2,1,0:T(8,128)(2,1)S(1)} %slice.441.refs_0_), channel_id=1, source_target_pairs={{0,12},{4,0},{8,4},{12,8},{16,28},{20,16},{24,20},{28,24},{32,44},... | collective-permute-start | bytes 884744 | tf_op jit(solution)/shard_map/ppermute | solution.py:225
  167.6 19.1 %collective-permute-start.40 = (bf16[256,1536]{1,0:T(8,128)(2,1)S(1)}, bf16[256,1536]{1,0:T(8,128)(2,1)S(1)}, u32[]{:S(2)}, u32[]{:S(2)}) collective-permute-start(bf16[256,1536]{1,0:T(8,128)(2,1)S(1)} %bitcast.302), channel_id=1, source_target_pairs={{0,32},{4,36},{8,40},{12,44},{16,48},{20,52},{24,56},{28,60},{32,6... | collective-permute-start | bytes 2359304 | tf_op jit(solution)/shard_map/ppermute | solution.py:231
  168.4 18.4 %collective-permute-start.41 = (bf16[256,1536]{1,0:T(8,128)(2,1)S(1)}, bf16[256,1536]{1,0:T(8,128)(2,1)S(1)}, u32[]{:S(2)}, u32[]{:S(2)}) collective-permute-start(bf16[256,1536]{1,0:T(8,128)(2,1)S(1)} %bitcast.303), channel_id=1, source_target_pairs={{0,96},{4,100},{8,104},{12,108},{16,112},{20,116},{24,120},{28,124... | collective-permute-start | bytes 2359304 | tf_op jit(solution)/shard_map/ppermute | solution.py:232
  171.4 25.4 %collective-permute-start.35 = (bf16[256,1024]{1,0:T(8,128)(2,1)S(1)}, bf16[256,1024]{1,0:T(8,128)(2,1)S(1)}, u32[]{:S(2)}, u32[]{:S(2)}) collective-permute-start(bf16[256,1024]{1,0:T(8,128)(2,1)S(1)} %multiply_convert_fusion.7), channel_id=1, source_target_pairs={{0,1},{1,0},{2,3},{3,2},{4,5},{5,4},{6,7},{7,6},{8,9},{9,8},{10,11... | collective-permute-start | bytes 1572872 | tf_op jit(solution)/shard_map/ppermute | solution.py:444
  204.0 24.8 %collective-permute-start.44 = (bf16[256,1024]{1,0:T(8,128)(2,1)}, bf16[256,1024]{1,0:T(8,128)(2,1)}, u32[]{:S(2)}, u32[]{:S(2)}) collective-permute-start(bf16[256,1024]{1,0:T(8,128)(2,1)} %convolution_convert_fusion.12), channel_id=1, source_target_pairs={{0,1},{1,0},{2,3},{3,2},{4,5},{5,4},{6,7},{7,6},{8,9},{9,8},{10,11... | collective-permute-start | bytes 1572872 | tf_op jit(solution)/shard_map/ppermute | solution.py:448
  204.0 22.7 %collective-permute-start.60 = (bf16[128,1024]{1,0:T(8,128)(2,1)}, bf16[128,1024]{1,0:T(8,128)(2,1)}, u32[]{:S(2)}, u32[]{:S(2)}) collective-permute-start(bf16[128,1024]{1,0:T(8,128)(2,1)} %param.16), channel_id=1, source_target_pairs={{0,2},{1,3},{2,0},{3,1},{4,6},{5,7},{6,4},{7,5},{8,10},{9,11},{10,... | collective-permute-start | bytes 786440 | tf_op jit(solution)/shard_map/ppermute | solution.py:437
  221.4 28.6 %collective-permute-start.50 = (bf16[256,1536]{1,0:T(8,128)(2,1)S(1)}, bf16[256,1536]{1,0:T(8,128)(2,1)S(1)}, u32[]{:S(2)}, u32[]{:S(2)}) collective-permute-start(bf16[256,1536]{1,0:T(8,128)(2,1)S(1)} %bitcast.260), channel_id=1, source_target_pairs={{0,4},{4,8},{8,12},{12,0},{16,20},{20,24},{24,28},{28,16},{32,36},... | collective-permute-start | bytes 2359304 | tf_op jit(solution)/shard_map/ppermute | solution.py:231
  225.3 25.5 %collective-permute-start.51 = (bf16[256,1536]{1,0:T(8,128)(2,1)S(1)}, bf16[256,1536]{1,0:T(8,128)(2,1)S(1)}, u32[]{:S(2)}, u32[]{:S(2)}) collective-permute-start(bf16[256,1536]{1,0:T(8,128)(2,1)S(1)} %bitcast.261), channel_id=1, source_target_pairs={{0,12},{4,0},{8,4},{12,8},{16,28},{20,16},{24,20},{28,24},{32,44},... | collective-permute-start | bytes 2359304 | tf_op jit(solution)/shard_map/ppermute | solution.py:232
  238.0 15.5 %collective-permute-start.45 = (bf16[256,1024]{1,0:T(8,128)(2,1)S(1)}, bf16[256,1024]{1,0:T(8,128)(2,1)S(1)}, u32[]{:S(2)}, u32[]{:S(2)}) collective-permute-start(bf16[256,1024]{1,0:T(8,128)(2,1)S(1)} %fusion.9), channel_id=1, source_target_pairs={{0,2},{1,3},{2,0},{3,1},{4,6},{5,7},{6,4},{7,5},{8,10},{9,11},{10,... | collective-permute-start | bytes 1572872 | tf_op jit(solution)/shard_map/ppermute | solution.py:453
  268.2 18.4 %collective-permute-start.58 = (bf16[256,1024]{1,0:T(8,128)(2,1)S(1)}, bf16[256,1024]{1,0:T(8,128)(2,1)S(1)}, u32[]{:S(2)}, u32[]{:S(2)}) collective-permute-start(bf16[256,1024]{1,0:T(8,128)(2,1)S(1)} %convolution_convert_fusion.16), channel_id=1, source_target_pairs={{0,1},{1,0},{2,3},{3,2},{4,5},{5,4},{6,7},{7,6},{8,9},{9,8},{10,11... | collective-permute-start | bytes 1572872 | tf_op jit(solution)/shard_map/ppermute | solution.py:448
  270.1 15.5 %collective-permute-start.63 = (bf16[256,1024]{1,0:T(8,128)(2,1)S(1)}, bf16[256,1024]{1,0:T(8,128)(2,1)S(1)}, u32[]{:S(2)}, u32[]{:S(2)}) collective-permute-start(bf16[256,1024]{1,0:T(8,128)(2,1)S(1)} %fusion.10), channel_id=1, source_target_pairs={{0,2},{1,3},{2,0},{3,1},{4,6},{5,7},{6,4},{7,5},{8,10},{9,11},{10,... | collective-permute-start | bytes 1572872 | tf_op jit(solution)/shard_map/ppermute | solution.py:453
  276.1 53.7 %collective-permute-start.82 = (bf16[8,32,2304]{2,1,0:T(8,128)(2,1)S(1)}, bf16[8,32,2304]{2,1,0:T(8,128)(2,1)S(1)}, u32[]{:S(2)}, u32[]{:S(2)}) collective-permute-start(bf16[8,32,2304]{2,1,0:T(8,128)(2,1)S(1)} %get-tuple-element.109), channel_id=1, source_target_pairs={{0,4},{4,8},{8,12},{12,0},{16,20},{20,24},{24,28},{28,16},{32,36},... | collective-permute-start | bytes 3538952 | tf_op jit(solution)/shard_map/ppermute | solution.py:348
  276.4 55.3 %collective-permute-start.83 = (bf16[8,32,2304]{2,1,0:T(8,128)(2,1)S(1)}, bf16[8,32,2304]{2,1,0:T(8,128)(2,1)S(1)}, u32[]{:S(2)}, u32[]{:S(2)}) collective-permute-start(bf16[8,32,2304]{2,1,0:T(8,128)(2,1)S(1)} %get-tuple-element.110), channel_id=1, source_target_pairs={{0,8},{4,12},{8,0},{12,4},{16,24},{20,28},{24,16},{28,20},{32,40},... | collective-permute-start | bytes 3538952 | tf_op jit(solution)/shard_map/ppermute | solution.py:348
  280.7 52.2 %collective-permute-start.84 = (bf16[8,32,2304]{2,1,0:T(8,128)(2,1)S(1)}, bf16[8,32,2304]{2,1,0:T(8,128)(2,1)S(1)}, u32[]{:S(2)}, u32[]{:S(2)}) collective-permute-start(bf16[8,32,2304]{2,1,0:T(8,128)(2,1)S(1)} %get-tuple-element.111), channel_id=1, source_target_pairs={{0,12},{4,0},{8,4},{12,8},{16,28},{20,16},{24,20},{28,24},{32,44},... | collective-permute-start | bytes 3538952 | tf_op jit(solution)/shard_map/ppermute | solution.py:348
  287.3 29.7 %collective-permute-start.59 = (bf16[128,1024]{1,0:T(8,128)(2,1)S(1)}, bf16[128,1024]{1,0:T(8,128)(2,1)S(1)}, u32[]{:S(2)}, u32[]{:S(2)}) collective-permute-start(bf16[128,1024]{1,0:T(8,128)(2,1)S(1)} %broadcast_select_fusion.7), channel_id=1, source_target_pairs={{0,2},{1,3},{2,0},{3,1},{4,6},{5,7},{6,4},{7,5},{8,10},{9,11},{10,... | collective-permute-start | bytes 786440 | tf_op jit(solution)/shard_map/ppermute | solution.py:462
  299.9 15.8 %collective-permute-start.66 = (bf16[256,1024]{1,0:T(8,128)(2,1)S(1)}, bf16[256,1024]{1,0:T(8,128)(2,1)S(1)}, u32[]{:S(2)}, u32[]{:S(2)}) collective-permute-start(bf16[256,1024]{1,0:T(8,128)(2,1)S(1)} %fusion.11), channel_id=1, source_target_pairs={{0,2},{1,3},{2,0},{3,1},{4,6},{5,7},{6,4},{7,5},{8,10},{9,11},{10,... | collective-permute-start | bytes 1572872 | tf_op jit(solution)/shard_map/ppermute | solution.py:453
  317.9 41.4 %collective-permute-start.79 = (bf16[256,1536]{1,0:T(8,128)(2,1)S(1)}, bf16[256,1536]{1,0:T(8,128)(2,1)S(1)}, u32[]{:S(2)}, u32[]{:S(2)}) collective-permute-start(bf16[256,1536]{1,0:T(8,128)(2,1)S(1)} %get-tuple-element.119), channel_id=1, source_target_pairs={{0,32},{4,36},{8,40},{12,44},{16,48},{20,52},{24,56},{28,60},{32,6... | collective-permute-start | bytes 2359304 | tf_op jit(solution)/shard_map/ppermute | solution.py:348
  323.8 37.1 %collective-permute-start.80 = (bf16[256,1536]{1,0:T(8,128)(2,1)S(1)}, bf16[256,1536]{1,0:T(8,128)(2,1)S(1)}, u32[]{:S(2)}, u32[]{:S(2)}) collective-permute-start(bf16[256,1536]{1,0:T(8,128)(2,1)S(1)} %get-tuple-element.120), channel_id=1, source_target_pairs={{0,64},{4,68},{8,72},{12,76},{16,80},{20,84},{24,88},{28,92},{32,9... | collective-permute-start | bytes 2359304 | tf_op jit(solution)/shard_map/ppermute | solution.py:348
  329.8 32.5 %collective-permute-start.81 = (bf16[256,1536]{1,0:T(8,128)(2,1)S(1)}, bf16[256,1536]{1,0:T(8,128)(2,1)S(1)}, u32[]{:S(2)}, u32[]{:S(2)}) collective-permute-start(bf16[256,1536]{1,0:T(8,128)(2,1)S(1)} %get-tuple-element.121), channel_id=1, source_target_pairs={{0,96},{4,100},{8,104},{12,108},{16,112},{20,116},{24,120},{28,124... | collective-permute-start | bytes 2359304 | tf_op jit(solution)/shard_map/ppermute | solution.py:348
  335.4 47.2 %collective-permute-start.90 = (bf16[8,32,1536]{2,1,0:T(8,128)(2,1)}, bf16[8,32,1536]{2,1,0:T(8,128)(2,1)}, u32[]{:S(2)}, u32[]{:S(2)}) collective-permute-start(bf16[8,32,1536]{2,1,0:T(8,128)(2,1)} %get-tuple-element.125), channel_id=1, source_target_pairs={{0,4},{4,8},{8,12},{12,0},{16,20},{20,24},{24,28},{28,16},{32,36},... | collective-permute-start | bytes 2359304 | tf_op jit(solution)/shard_map/ppermute | solution.py:348
  349.8 34.4 %collective-permute-start.91 = (bf16[8,32,1536]{2,1,0:T(8,128)(2,1)}, bf16[8,32,1536]{2,1,0:T(8,128)(2,1)}, u32[]{:S(2)}, u32[]{:S(2)}) collective-permute-start(bf16[8,32,1536]{2,1,0:T(8,128)(2,1)} %get-tuple-element.126), channel_id=1, source_target_pairs={{0,8},{4,12},{8,0},{12,4},{16,24},{20,28},{24,16},{28,20},{32,40},... | collective-permute-start | bytes 2359304 | tf_op jit(solution)/shard_map/ppermute | solution.py:348
  359.4 41.5 %collective-permute-start.92 = (bf16[8,32,1536]{2,1,0:T(8,128)(2,1)}, bf16[8,32,1536]{2,1,0:T(8,128)(2,1)}, u32[]{:S(2)}, u32[]{:S(2)}) collective-permute-start(bf16[8,32,1536]{2,1,0:T(8,128)(2,1)} %get-tuple-element.127), channel_id=1, source_target_pairs={{0,12},{4,0},{8,4},{12,8},{16,28},{20,16},{24,20},{28,24},{32,44},... | collective-permute-start | bytes 2359304 | tf_op jit(solution)/shard_map/ppermute | solution.py:348
  360.9 82.4 %collective-permute-start.85 = (bf16[128,2304]{1,0:T(8,128)(2,1)}, bf16[128,2304]{1,0:T(8,128)(2,1)}, u32[]{:S(2)}, u32[]{:S(2)}) collective-permute-start(bf16[128,2304]{1,0:T(8,128)(2,1)} %bitcast.87), channel_id=1, source_target_pairs={{0,16},{4,20},{8,24},{12,28},{16,0},{20,4},{24,8},{28,12},{32,48},... | collective-permute-start | bytes 1769480 | tf_op jit(solution)/shard_map/ppermute | solution.py:377
  366.4 76.8 %collective-permute-start.86 = (bf16[128,1536]{1,0:T(8,128)(2,1)}, bf16[128,1536]{1,0:T(8,128)(2,1)}, u32[]{:S(2)}, u32[]{:S(2)}) collective-permute-start(bf16[128,1536]{1,0:T(8,128)(2,1)} %broadcast_select_fusion.4), channel_id=1, source_target_pairs={{0,16},{4,20},{8,24},{12,28},{16,0},{20,4},{24,8},{28,12},{32,48},... | collective-permute-start | bytes 1179656 | tf_op jit(solution)/shard_map/ppermute | solution.py:377
  374.1 105.2 %all-to-all-start = ((bf16[32,32,1280]{2,1,0:T(8,128)(2,1)}), bf16[32,32,1280]{2,1,0:T(8,128)(2,1)}, u32[]{:S(2)}, u32[]{:S(2)}) async-start(bf16[32,32,1280]{2,1,0:T(8,128)(2,1)} %pad_maximum_fusion), calls=%async_computation | async-start | bytes 5242880 | tf_op jit(solution)/shard_map/all_to_all | solution.py:496
  382.6 46.2 %collective-permute-start.75 = (bf16[256,1280]{1,0:T(8,128)(2,1)S(1)}, bf16[256,1280]{1,0:T(8,128)(2,1)S(1)}, u32[]{:S(2)}, u32[]{:S(2)}) collective-permute-start(bf16[256,1280]{1,0:T(8,128)(2,1)S(1)} %copy-done.54), channel_id=1, source_target_pairs={{0,32},{4,36},{8,40},{12,44},{16,48},{20,52},{24,56},{28,60},{32,6... | collective-permute-start | bytes 1966088 | tf_op jit(solution)/shard_map/ppermute | solution.py:348
  384.2 58.3 %collective-permute-start.76 = (bf16[256,1280]{1,0:T(8,128)(2,1)S(1)}, bf16[256,1280]{1,0:T(8,128)(2,1)S(1)}, u32[]{:S(2)}, u32[]{:S(2)}) collective-permute-start(bf16[256,1280]{1,0:T(8,128)(2,1)S(1)} %copy-done.52), channel_id=1, source_target_pairs={{0,64},{4,68},{8,72},{12,76},{16,80},{20,84},{24,88},{28,92},{32,9... | collective-permute-start | bytes 1966088 | tf_op jit(solution)/shard_map/ppermute | solution.py:348
  400.8 42.0 %collective-permute-start.77 = (bf16[256,1280]{1,0:T(8,128)(2,1)S(1)}, bf16[256,1280]{1,0:T(8,128)(2,1)S(1)}, u32[]{:S(2)}, u32[]{:S(2)}) collective-permute-start(bf16[256,1280]{1,0:T(8,128)(2,1)S(1)} %copy-done.50), channel_id=1, source_target_pairs={{0,96},{4,100},{8,104},{12,108},{16,112},{20,116},{24,120},{28,124... | collective-permute-start | bytes 1966088 | tf_op jit(solution)/shard_map/ppermute | solution.py:348
  428.8 18.6 %collective-permute-start.72 = (bf16[128,1024]{1,0:T(8,128)(2,1)S(1)}, bf16[128,1024]{1,0:T(8,128)(2,1)S(1)}, u32[]{:S(2)}, u32[]{:S(2)}) collective-permute-start(bf16[128,1024]{1,0:T(8,128)(2,1)S(1)} %broadcast_select_fusion.8), channel_id=1, source_target_pairs={{0,2},{1,3},{2,0},{3,1},{4,6},{5,7},{6,4},{7,5},{8,10},{9,11},{10,... | collective-permute-start | bytes 786440 | tf_op jit(solution)/shard_map/ppermute | solution.py:462
  443.3 16.1 %collective-permute-start.78 = (bf16[128,1280]{1,0:T(8,128)(2,1)S(1)}, bf16[128,1280]{1,0:T(8,128)(2,1)S(1)}, u32[]{:S(2)}, u32[]{:S(2)}) collective-permute-start(bf16[128,1280]{1,0:T(8,128)(2,1)S(1)} %broadcast_select_fusion.5), channel_id=1, source_target_pairs={{0,16},{4,20},{8,24},{12,28},{16,0},{20,4},{24,8},{28,12},{32,48},... | collective-permute-start | bytes 983048 | tf_op jit(solution)/shard_map/ppermute | solution.py:377
  (145 other events, 1185.8 us)
